TPU v7x, 256 devices: a whole 4x4x8 slice. The times are simulated.
256 devices in a mesh: grp: 8 (over z), var: 32 (over x, y, core).
Axes of the slice: x: 4, y: 4, z: 8, core: 2. Of those that a mesh axis runs over, the one named last changes fastest.
Arguments:
- series: bfloat16 [8, 2048, 64, 128], P('grp', 'var'), parts along dimension 0, may hold values from -12 to 12
- sensor_total_count: int32 [8], P('grp'), parts along dimension 0, may hold values from 1024 to 2048
- depthwise_weight: bfloat16 [2048, 64, 51], P('var'), may hold values from -0.875 to 0.875
- batchnorm_gain: float32 [64], replicated, may hold values from 0.5 to 1.5
- batchnorm_bias: float32 [64], replicated, may hold values from -2 to 2
- channel_up_weight: bfloat16 [2048, 64, 256], P('var'), may hold values from -0.75 to 0.75
- channel_down_weight: bfloat16 [2048, 256, 64], P('var'), may hold values from -0.375 to 0.375
- down_factor1: bfloat16 [64, 8], replicated, may hold values from -0.75 to 0.75
- up_factor1: bfloat16 [8, 256], replicated, may hold values from -2 to 2
- sensor_up_weight: bfloat16 [64, 2048, 256], P('var'), may hold values from -0.125 to 0.125
- sensor_down_weight: bfloat16 [64, 256, 2048], P('var'), may hold values from -0.375 to 0.375
- down_factor2: bfloat16 [2048, 8], replicated, may hold values from -0.125 to 0.125
- up_factor2: bfloat16 [8, 256], replicated, may hold values from -2 to 2
- upstream: bfloat16 [8, 2048, 64, 128], P('grp', 'var'), parts along dimension 0, may hold values from -0.01171875 to 0.01171875
Outputs:
- mixed: bfloat16 [8, 2048, 64, 128], P('grp', 'var'), parts along dimension 0
- gradient_down_factor1: float32 [512, 8], P('grp'), parts along dimension 0
- gradient_up_factor1: float32 [64, 256], P('grp'), parts along dimension 0
- gradient_down_factor2: float32 [16384, 8], P('grp'), parts along dimension 0
- gradient_up_factor2: float32 [64, 256], P('grp'), parts along dimension 0
There are 8 independent parts, one for each index of `grp`. A program takes and returns all parts, laid end to end along the dimension named above; an argument that names none is the same for every part. Nothing has to cross between parts.
All inputs are finite; a program needn't handle non-finite values.
Results may differ from a plain program's by a relative error of at most 0.028.
Values may be sent and summed in bfloat16 or wider, within the bound.
A program may use at most 128 MiB of HBM per device.

v0:
```python
import jax
import jax.numpy as jnp
from jax import lax
from jax.sharding import PartitionSpec as P

tanh_scale = 0.7978845608028654
cubic_term = 0.044715


def gelu_value(values):
    return (
        0.5
        * values
        * (1.0 + jnp.tanh(tanh_scale * (values + cubic_term * values * values * values)))
    )


def gelu_slope(values):
    inner = jnp.tanh(tanh_scale * (values + cubic_term * values * values * values))
    return 0.5 * (1.0 + inner) + 0.5 * values * (1.0 - inner * inner) * tanh_scale * (
        1.0 + 3.0 * cubic_term * values * values
    )


def depthwise(series, depthwise_weight):
    batch_count, sensors, channels, patches = series.shape
    tap_count = depthwise_weight.shape[-1]
    stacked = series.reshape(batch_count, sensors * channels, patches)
    kernel = depthwise_weight.reshape(sensors * channels, 1, tap_count)
    result = lax.conv_general_dilated(
        stacked,
        kernel,
        (1,),
        [(tap_count // 2, tap_count // 2)],
        dimension_numbers=("NCH", "OIH", "NCH"),
        feature_group_count=sensors * channels,
        preferred_element_type=jnp.float32,
    )
    return result.reshape(batch_count, sensors, channels, patches)


def mixing_forward(input_rows, sensor_up_weight, sensor_down_weight, down_factor2, up_factor2):
    second_rank_projection = jnp.einsum(
        "zjol,jy->zoly", input_rows, down_factor2, preferred_element_type=jnp.float32
    ).astype(jnp.bfloat16)
    second_preactivation = jnp.einsum(
        "pfyr,yfe->pyre", input_rows, sensor_up_weight, preferred_element_type=jnp.float32
    ) + jnp.einsum(
        "iezo,ot->iezt", second_rank_projection, up_factor2, preferred_element_type=jnp.float32
    )
    hidden_two = gelu_value(second_preactivation).astype(jnp.bfloat16)
    mixed_two = jnp.einsum(
        "bdnj,djm->bmdn", hidden_two, sensor_down_weight, preferred_element_type=jnp.float32
    ).astype(jnp.bfloat16)
    return (mixed_two, second_preactivation, second_rank_projection)


def mix_backward(
    input_rows,
    output_gradient,
    second_preactivation,
    second_rank_projection,
    complete_sensor_mask,
    sensor_up_weight,
    sensor_down_weight,
    down_factor2,
    up_factor2,
):
    masked = output_gradient * complete_sensor_mask[None, :, None, None]
    grad_hidden = jnp.einsum(
        "bmdn,djm->bdnj", masked, sensor_down_weight, preferred_element_type=jnp.float32
    )
    preactivation_gradient = (grad_hidden * gelu_slope(second_preactivation)).astype(jnp.bfloat16)
    backward_second = jnp.einsum(
        "gywi,xi->gywx", preactivation_gradient, up_factor2, preferred_element_type=jnp.float32
    ).astype(jnp.bfloat16)
    item_b2 = jnp.einsum(
        "bdnr,bdnj->brj",
        second_rank_projection,
        preactivation_gradient,
        preferred_element_type=jnp.float32,
    )
    item_a2 = jnp.einsum(
        "bmdn,bdnr->brm", input_rows, backward_second, preferred_element_type=jnp.float32
    )
    grad_feat = jnp.einsum(
        "whgl,htl->wthg",
        preactivation_gradient,
        sensor_up_weight,
        preferred_element_type=jnp.float32,
    ) + jnp.einsum(
        "apej,kj->akpe", backward_second, down_factor2, preferred_element_type=jnp.float32
    )
    return (grad_feat.astype(jnp.bfloat16), item_b2, item_a2)


def body(
    series,
    sensor_total_count,
    depthwise_weight,
    batchnorm_gain,
    batchnorm_bias,
    channel_up_weight,
    channel_down_weight,
    down_factor1,
    up_factor1,
    sensor_up_weight,
    sensor_down_weight,
    down_factor2,
    up_factor2,
    upstream,
):
    batch_count, local_vars, channels, patches = series.shape
    whole_vars = sensor_up_weight.shape[1]
    live_limit = sensor_total_count[0]
    first_var = lax.axis_index("var") * local_vars
    local_live = (first_var + jnp.arange(local_vars, dtype=jnp.int32) < live_limit).astype(
        jnp.float32
    )
    complete_sensor_mask = (jnp.arange(whole_vars, dtype=jnp.int32) < live_limit).astype(
        jnp.bfloat16
    )
    live_mask = local_live[None, :, None, None]
    live_total = live_limit.astype(jnp.float32) * (batch_count * patches)
    convolved = depthwise(series, depthwise_weight)
    weighted = convolved * live_mask
    moment_one, moment_two = lax.psum(
        (jnp.sum(weighted, axis=(0, 1, 3)), jnp.sum(weighted * convolved, axis=(0, 1, 3))), "var"
    )
    bn_mean = moment_one / live_total
    spread = moment_two / live_total - bn_mean * bn_mean
    bn_scale = batchnorm_gain * lax.rsqrt(spread + 1e-05)
    shifted = (convolved - bn_mean[None, None, :, None]) * bn_scale[
        None, None, :, None
    ] + batchnorm_bias[None, None, :, None]
    normalized_rows = (shifted * live_mask).astype(jnp.bfloat16)
    first_rank_projection = jnp.einsum(
        "tkie,if->tkfe", normalized_rows, down_factor1, preferred_element_type=jnp.float32
    ).astype(jnp.bfloat16)
    first_preactivation = jnp.einsum(
        "wlqk,lqz->wlzk", normalized_rows, channel_up_weight, preferred_element_type=jnp.float32
    ) + jnp.einsum(
        "pkui,uv->pkvi", first_rank_projection, up_factor1, preferred_element_type=jnp.float32
    )
    first_hidden_state = gelu_value(first_preactivation).astype(jnp.bfloat16)
    input_rows = jnp.einsum(
        "uweg,wel->uwlg",
        first_hidden_state,
        channel_down_weight,
        preferred_element_type=jnp.float32,
    ).astype(jnp.bfloat16)
    output_pieces = lax.all_to_all(input_rows, "var", split_axis=2, concat_axis=1, tiled=True)
    mixed_two, second_preactivation, second_rank_projection, swapped_axes = mixing_forward(
        output_pieces, sensor_up_weight, sensor_down_weight, down_factor2, up_factor2
    ) + (output_pieces,)
    output_gradient = lax.all_to_all(upstream, "var", split_axis=2, concat_axis=1, tiled=True)
    grad_feat, item_b2, item_a2 = mix_backward(
        swapped_axes,
        output_gradient,
        second_preactivation,
        second_rank_projection,
        complete_sensor_mask,
        sensor_up_weight,
        sensor_down_weight,
        down_factor2,
        up_factor2,
    )
    mixed_back, backward_gradient = (
        lax.all_to_all(mixed_two, "var", split_axis=1, concat_axis=2, tiled=True),
        lax.all_to_all(grad_feat, "var", split_axis=1, concat_axis=2, tiled=True),
    )
    mixed = (series.astype(jnp.float32) + live_mask * mixed_back.astype(jnp.float32)).astype(
        jnp.bfloat16
    )
    first_hidden_gradient = jnp.einsum(
        "zyof,ylo->zylf", backward_gradient, channel_down_weight, preferred_element_type=jnp.float32
    )
    first_preactivation_gradient = (first_hidden_gradient * gelu_slope(first_preactivation)).astype(
        jnp.bfloat16
    )
    part_b1 = jnp.einsum(
        "udls,udks->lk",
        first_rank_projection,
        first_preactivation_gradient,
        preferred_element_type=jnp.float32,
    )
    backward_first = jnp.einsum(
        "otzf,gz->otgf",
        first_preactivation_gradient,
        up_factor1,
        preferred_element_type=jnp.float32,
    ).astype(jnp.bfloat16)
    part_a1 = jnp.einsum(
        "cvsw,cvow->so", normalized_rows, backward_first, preferred_element_type=jnp.float32
    )
    part_b2 = jnp.sum(item_b2, axis=0)
    part_a2 = jnp.sum(item_a2, axis=0)
    grad_a1, grad_b1, grad_a2_rows, grad_b2 = (
        lax.psum(part_a1.astype(jnp.bfloat16), "var").astype(jnp.float32),
        lax.psum(part_b1.astype(jnp.bfloat16), "var").astype(jnp.float32),
        lax.psum(part_a2.astype(jnp.bfloat16), "var").astype(jnp.float32),
        lax.psum(part_b2.astype(jnp.bfloat16), "var").astype(jnp.float32),
    )
    return (mixed, grad_a1, grad_b1, grad_a2_rows.T, grad_b2)


def solution(mesh):
    placed = (
        P("grp", "var", None, None),
        P("grp"),
        P("var", None, None),
        P(),
        P(),
        P("var", None, None),
        P("var", None, None),
        P(),
        P(),
        P("var", None, None),
        P("var", None, None),
        P(),
        P(),
        P("grp", "var", None, None),
    )
    return jax.shard_map(
        body,
        mesh=mesh,
        in_specs=placed,
        out_specs=(
            P("grp", "var", None, None),
            P("grp", None),
            P("grp", None),
            P("grp", None),
            P("grp", None),
        ),
        check_vma=False,
    )
```

profile of v0, /device:TPU:1, one launch (start us, length us, event | category | flops | bytes accessed | tf_op | source)
XLA Modules:
  0.0 337.6 jit_solution(12600948008213310835)
XLA Ops:
  0.6 3.1 copy.139
  3.8 8.8 %all-to-all-start.2 = ((bf16[1,64,64,128]{3,1,0,2:T(8,128)(2,1)}), bf16[1,64,64,128]{3,1,0,2:T(8,128)(2,1)}, u32[]{:S(2)}, u32[]{:S(2)}) async-start(bf16[1,64,64,128]{3,1,0,2:T(8,128)(2,1)} %copy.139), calls=%async_computation.2 | async-start | bytes 2097152 | tf_op jit(solution)/shard_map/all_to_all | solution.py:156
  13.4 3.9 %reshape.190 = bf16[4096,1,51]{0,1,2:T(2,128)(2,1)} reshape(bf16[64,64,51]{1,0,2:T(8,128)(2,1)} %param.16) | data formatting | bytes 835584 | tf_op jit(solution)/shard_map/reshape | solution.py:29
  17.2 4.2 %copy.126 = bf16[1,4096,128]{1,0,2:T(2,128)(2,1)} copy(bf16[1,4096,128]{2,1,0:T(8,128)(2,1)S(1)} %bitcast.208) | data formatting | bytes 2097152 | tf_op jit(solution)/shard_map/reshape | solution.py:28
  21.5 16.3 %fusion.80 = f32[1,4096,128]{1,0,2:T(1,128)} fusion(bf16[1,4096,128]{1,0,2:T(2,128)(2,1)} %copy.126, bf16[4096,1,51]{0,1,2:T(2,128)(2,1)} %reshape.190), kind=kOutput, calls=%fused_computation.90 | convolution fusion | flops 48152576 | bytes 3563520 | tf_op jit(solution)/shard_map/conv_general_dilated | solution.py:30
  37.7 5.7 %copy.128 = f32[1,4096,128]{2,1,0:T(8,128)} copy(f32[1,4096,128]{1,0,2:T(1,128)} %fusion.80) | data formatting | bytes 4194304 | tf_op jit(solution)/shard_map/conv_general_dilated | solution.py:30
  43.4 3.1 fusion.18
  46.7 62.5 %all-reduce = (f32[64]{0:T(128)S(1)}, f32[64]{0:T(128)S(1)}) all-reduce(f32[64]{0:T(128)S(1)} %reduce_sum.42, f32[64]{0:T(128)S(1)} %reduce_sum.45), channel_id=1, replica_groups=mesh['grp'=8,'var'=32] {'var'}, use_global_device_ids=true, to_apply=%region_2.0 | all-reduce | flops 128 | bytes 1024 | tf_op jit(solution)/shard_map/psum | solution.py:127
  109.2 3.1 multiply_convert_fusion.3
  115.2 3.3 fusion.22
  120.2 8.9 %all-to-all-start = ((bf16[1,64,64,128]{3,1,0,2:T(8,128)(2,1)}), bf16[1,64,64,128]{3,1,0,2:T(8,128)(2,1)S(1)}, u32[]{:S(2)}, u32[]{:S(2)}) async-start(bf16[1,64,64,128]{3,1,0,2:T(8,128)(2,1)} %copy.132), calls=%async_computation | async-start | bytes 2097152 | tf_op jit(solution)/shard_map/all_to_all | solution.py:152
  129.4 5.9 %multiply_convert_fusion.2 = bf16[1,4096,128]{2,1,0:T(8,128)(2,1)} fusion(f32[1,4096,128]{2,1,0:T(8,128)} %copy.128, f32[4096]{0:T(1024)S(1)} %add.104, f32[4096]{0:T(1024)S(1)} %mul.228, f32[4096]{0:T(1024)S(1)} %sub.35, f32[4096]{0:T(1024)S(1)} %mul.203), kind=kLoop, calls=%fused_computation.30 | loop fusion | flops 2621440 | bytes 3211264 | tf_op jit(solution)/shard_map/convert_element_type | solution.py:136
  135.3 2.3 copy.140
  137.6 8.5 %all-to-all-done = bf16[1,64,64,128]{3,1,0,2:T(8,128)(2,1)S(1)} async-done(((bf16[1,64,64,128]{3,1,0,2:T(8,128)(2,1)}), bf16[1,64,64,128]{3,1,0,2:T(8,128)(2,1)S(1)}, u32[]{:S(2)}, u32[]{:S(2)}) %all-to-all-start) | async-done | bytes 1048608 | tf_op jit(solution)/shard_map/all_to_all | solution.py:152
  152.1 3.7 %copy.135 = bf16[1,2048,2,128]{3,2,0,1:T(2,128)(2,1)} copy(bf16[1,2048,2,128]{1,3,2,0:T(8,128)(2,1)} %fusion.15) | data formatting | bytes 2097152 | tf_op jit(solution)/shard_map/convert_element_type | solution.py:54
  155.7 4.5 %all-to-all-start.1 = ((bf16[1,2048,2,128]{3,2,0,1:T(2,128)(2,1)}), bf16[1,2048,2,128]{3,2,0,1:T(2,128)(2,1)}, u32[]{:S(2)}, u32[]{:S(2)}) async-start(bf16[1,2048,2,128]{3,2,0,1:T(2,128)(2,1)} %copy.135), calls=%async_computation.1 | async-start | bytes 2097152 | tf_op jit(solution)/shard_map/all_to_all | solution.py:169
  160.2 3.1 fusion.38
  165.8 3.7 %copy.142 = bf16[1,2048,2,128]{3,2,0,1:T(2,128)(2,1)} copy(bf16[1,2048,2,128]{1,3,2,0:T(8,128)(2,1)} %fusion.14) | data formatting | bytes 2097152 | tf_op jit(solution)/shard_map/convert_element_type | solution.py:94
  169.4 7.7 %all-to-all-done.1 = bf16[1,2048,2,128]{3,2,0,1:T(2,128)(2,1)} async-done(((bf16[1,2048,2,128]{3,2,0,1:T(2,128)(2,1)}), bf16[1,2048,2,128]{3,2,0,1:T(2,128)(2,1)}, u32[]{:S(2)}, u32[]{:S(2)}) %all-to-all-start.1) | async-done | bytes 1048608 | tf_op jit(solution)/shard_map/all_to_all | solution.py:169
  177.2 4.5 %all-to-all-start.3 = ((bf16[1,2048,2,128]{3,2,0,1:T(2,128)(2,1)}), bf16[1,2048,2,128]{3,2,0,1:T(2,128)(2,1)}, u32[]{:S(2)}, u32[]{:S(2)}) async-start(bf16[1,2048,2,128]{3,2,0,1:T(2,128)(2,1)} %copy.142), calls=%async_computation.3 | async-start | bytes 2097152 | tf_op jit(solution)/shard_map/all_to_all | solution.py:170
  187.4 11.2 %all-to-all-done.3 = bf16[1,2048,2,128]{3,2,0,1:T(2,128)(2,1)} async-done(((bf16[1,2048,2,128]{3,2,0,1:T(2,128)(2,1)}), bf16[1,2048,2,128]{3,2,0,1:T(2,128)(2,1)}, u32[]{:S(2)}, u32[]{:S(2)}) %all-to-all-start.3) | async-done | bytes 1048608 | tf_op jit(solution)/shard_map/all_to_all | solution.py:170
  201.1 8.0 %fusion.6 = bf16[1,64,256,128]{2,3,1,0:T(8,128)(2,1)S(1)} fusion(f32[1,64,256,128]{2,3,1,0:T(8,128)} %copy-done.2, bf16[64,64,128]{2,1,0:T(8,128)(2,1)S(1)} %bitcast.214, bf16[64,256,64]{1,2,0:T(8,128)(2,1)S(1)} %copy-done), kind=kOutput, calls=%fused_computation.8 | convolution fusion | flops 308281344 | bytes 15728640 | tf_op jit(solution)/shard_map/zyof,ylo->zylf/dot_general | solution.py:175
  211.1 3.7 %fusion.49 = bf16[64,8]{0,1:T(8,128)(2,1)S(1)} fusion(bf16[64,64,128]{2,1,0:T(8,128)(2,1)S(1)} %bitcast.210, bf16[1,64,256,128]{2,3,1,0:T(8,128)(2,1)} %copy-done.1, bf16[8,256]{1,0:T(8,128)(2,1)S(1)} %copy-done.14), kind=kOutput, calls=%fused_computation.54 | convolution fusion | flops 42009088 | bytes 5248000 | tf_op jit(solution)/shard_map/cvsw,cvow->so/dot_general | solution.py:193
  214.9 120.4 %all-reduce.1 = (bf16[64,8]{0,1:T(8,128)(2,1)S(1)}, bf16[8,256]{1,0:T(8,128)(2,1)S(1)}, bf16[2048,8]{0,1:T(8,128)(2,1)S(1)}, bf16[8,256]{1,0:T(8,128)(2,1)S(1)}) all-reduce(bf16[64,8]{0,1:T(8,128)(2,1)S(1)} %fusion.49, bf16[8,256]{1,0:T(8,128)(2,1)S(1)} %fusion.43, ...), channel_id=1, replica_groups=mesh['grp'=8,'var'=32] {'var'}, use_global_device_ids=true, to_apply=%region_6.0 | all-reduce | flops 20992 | bytes 83968 | tf_op jit(solution)/shard_map/psum | solution.py:199
  (78 shorter events, 26.1 us)
Async XLA Ops:
  0.6 114.6 %copy-start = (bf16[64,256,64]{1,2,0:T(8,128)(2,1)S(1)}, bf16[64,256,64]{1,2,0:T(8,128)(2,1)}, u32[]{:S(2)}) copy-start(bf16[64,256,64]{1,2,0:T(8,128)(2,1)} %param.20) | copy-start | bytes 6291460
  3.8 13.5 %copy-start.5 = (bf16[1,64,64,128]{3,2,1,0:T(8,128)(2,1)S(1)}, bf16[1,64,64,128]{3,2,1,0:T(8,128)(2,1)}, u32[]{:S(2)}) copy-start(bf16[1,64,64,128]{3,2,1,0:T(8,128)(2,1)} %param.14) | copy-start | bytes 3145732
  3.8 116.4 %all-to-all-start.2 = ((bf16[1,64,64,128]{3,1,0,2:T(8,128)(2,1)}), bf16[1,64,64,128]{3,1,0,2:T(8,128)(2,1)}, u32[]{:S(2)}, u32[]{:S(2)}) async-start(bf16[1,64,64,128]{3,1,0,2:T(8,128)(2,1)} %copy.139), calls=%async_computation.2 | async-start | bytes 2097152 | tf_op jit(solution)/shard_map/all_to_all | solution.py:156
  43.4 65.8 %copy-start.17 = (f32[64]{0:T(128)S(1)}, f32[64]{0:T(128)}, u32[]{:S(2)}) copy-start(f32[64]{0:T(128)} %param.17) | copy-start | bytes 772
  43.4 65.8 %copy-start.16 = (f32[64]{0:T(128)S(1)}, f32[64]{0:T(128)}, u32[]{:S(2)}) copy-start(f32[64]{0:T(128)} %param.18) | copy-start | bytes 772
  46.5 65.9 %copy-start.15 = (bf16[64,8]{0,1:T(8,128)(2,1)S(1)}, bf16[64,8]{0,1:T(8,128)(2,1)}, u32[]{:S(2)}) copy-start(bf16[64,8]{0,1:T(8,128)(2,1)} %param.21) | copy-start | bytes 3076
  109.2 3.4 copy-start.10
  112.6 1.3 copy-start.14
  115.2 3.3 copy-start.2
  120.2 25.9 %all-to-all-start = ((bf16[1,64,64,128]{3,1,0,2:T(8,128)(2,1)}), bf16[1,64,64,128]{3,1,0,2:T(8,128)(2,1)S(1)}, u32[]{:S(2)}, u32[]{:S(2)}) async-start(bf16[1,64,64,128]{3,1,0,2:T(8,128)(2,1)} %copy.132), calls=%async_computation | async-start | bytes 2097152 | tf_op jit(solution)/shard_map/all_to_all | solution.py:152
  135.3 13.2 %copy-start.12 = (bf16[2048,8]{0,1:T(8,128)(2,1)S(1)}, bf16[2048,8]{0,1:T(8,128)(2,1)}, u32[]{:S(2)}) copy-start(bf16[2048,8]{0,1:T(8,128)(2,1)} %param.25) | copy-start | bytes 98308
  146.1 1.0 copy-start.8
  147.1 1.9 copy-start.3
  148.5 1.0 copy-start.13
  149.0 1.6 copy-start.9
  149.8 0.7 copy-start.11
  155.7 21.4 %all-to-all-start.1 = ((bf16[1,2048,2,128]{3,2,0,1:T(2,128)(2,1)}), bf16[1,2048,2,128]{3,2,0,1:T(2,128)(2,1)}, u32[]{:S(2)}, u32[]{:S(2)}) async-start(bf16[1,2048,2,128]{3,2,0,1:T(2,128)(2,1)} %copy.135), calls=%async_computation.1 | async-start | bytes 2097152 | tf_op jit(solution)/shard_map/all_to_all | solution.py:169
  160.2 3.1 copy-start.4
  177.2 21.4 %all-to-all-start.3 = ((bf16[1,2048,2,128]{3,2,0,1:T(2,128)(2,1)}), bf16[1,2048,2,128]{3,2,0,1:T(2,128)(2,1)}, u32[]{:S(2)}, u32[]{:S(2)}) async-start(bf16[1,2048,2,128]{3,2,0,1:T(2,128)(2,1)} %copy.142), calls=%async_computation.3 | async-start | bytes 2097152 | tf_op jit(solution)/shard_map/all_to_all | solution.py:170
  183.8 1.2 copy-start.6
  209.1 2.0 copy-start.1
  209.1 2.0 copy-start.7
where the time goes:
time: 343 us; the launch traced here: 338 us
  blocking collectives  183 us (53%)
  matrix products  43.4 us (13%)
  local copies, waits for them, and re-layouts  40.1 us (12%)
  waiting for transfers between devices  27.4 us (8%)
  starting transfers between devices  26.6 us (8%)
  other arithmetic  15.5 us (5%)
    psum x1, blocking collectives, body(): lax.psum(part_a1.astype(jnp.bfloat16), 'var').astype(jnp.float32)  120 us
    psum x1, blocking collectives, body(): lax.psum((jnp.sum(weighted, axis=(0, 1, 3)), jnp.sum(weighted * convolved...  62.5 us
    conv_general_dilated x1, matrix products, depthwise(): lax.conv_general_dilated(stacked, kernel, (1,), [(tap_count // 2, tap_cou...  16.3 us
    all_to_all x1, waiting for transfers between devices, body(): lax.all_to_all(grad_feat, 'var', split_axis=1, concat_axis=2, tiled=True)  11.2 us
    unnamed x38, local copies, waits for them, and re-layouts  9.05 us
    convert_element_type x2, other arithmetic, body(): normalized_rows = (shifted * live_mask).astype(jnp.bfloat16)  9.01 us
    all_to_all x1, starting transfers between devices, body(): lax.all_to_all(input_rows, 'var', split_axis=2, concat_axis=1, tiled=True)  8.93 us
    all_to_all x1, starting transfers between devices, body(): lax.all_to_all(upstream, 'var', split_axis=2, concat_axis=1, tiled=True)  8.77 us
  transfers between devices with their start and end apart: 4, of which 3 were waited for; matrix products, arithmetic and copies ran while one was open for 20% of the time, Pallas kernels for 0%

commit v1 on v0

v1 whole, which is shorter than its diff:
```python
import jax
import jax.numpy as jnp
from jax import lax
from jax.experimental import pallas as pl
from jax.experimental.pallas import tpu as pltpu
from jax.sharding import PartitionSpec as P

F32 = jnp.float32
BF16 = jnp.bfloat16
MESH = pl.DeviceIdType.MESH

tanh_scale = 0.7978845608028654
cubic_term = 0.044715

PEERS = 32
SENSORS = 64
CHANNELS = 64
PATCHES = 128
TAPS = 51
HALF = TAPS // 2
GROUPS = 4
PADDED = PATCHES + 2 * HALF
SLOTS = PEERS * SENSORS
HIDDEN = 256
OWN = 2
CHUNKS = 2
CHUNK = SENSORS // CHUNKS
BLOCK = 16


def gelu_parts(v):
    square = v * v
    half = 0.5 * jnp.tanh(v * (tanh_scale + (tanh_scale * cubic_term) * square)) + 0.5
    value = v * half
    slope = half + (value * (1.0 - half)) * (
        2.0 * tanh_scale + (6.0 * tanh_scale * cubic_term) * square
    )
    return value, slope


def dot(a, b, contract=((1,), (0,))):
    return lax.dot_general(a, b, (contract, ((), ())), preferred_element_type=F32)


NT = ((1,), (1,))
TN = ((0,), (0,))


def offset_peer(me, offset, sign):
    x, y, c = me // 8, (me // 2) % 4, me % 2
    dx, dy, dc = offset // 8, (offset // 2) % 4, offset % 2
    return (
        ((x + 4 + sign * dx) % 4) * 8 + ((y + 4 + sign * dy) % 4) * 2 + (c + 2 + sign * dc) % 2
    )


def offset_of(me, peer):
    dx = (peer // 8 + 4 - me // 8) % 4
    dy = ((peer // 2) % 4 + 4 - (me // 2) % 4) % 4
    dc = (peer % 2 + 2 - me % 2) % 2
    return dx * 8 + dy * 2 + dc


def kernel(
    count_ref,
    gain_ref,
    bias_ref,
    df1_ref,
    uf1_ref,
    df2_ref,
    uf2_ref,
    series_hbm,
    taps_hbm,
    up1_hbm,
    down1_hbm,
    up2_hbm,
    down2_hbm,
    upstream_hbm,
    mixed_hbm,
    gd1_ref,
    gu1_ref,
    gd2_ref,
    gu2_ref,
    series,
    taps,
    up1,
    down1,
    up2,
    down2,
    upstream,
    padded,
    packed_taps,
    conv,
    rows32,
    normed_ref,
    low_t,
    slope_ref,
    u_send,
    u_recv,
    f_send,
    f_recv,
    g_send,
    g_recv,
    m_send,
    m_recv,
    out_buf,
    st_send,
    st_recv,
    dft,
    ufr,
    gh_ref,
    hid_ref,
    gp2_ref,
    back_ref,
    part,
    part_recv,
    total,
    total_recv,
    load_sems,
    self_sems,
    u_ssem,
    u_rsem,
    st_ssem,
    st_rsem,
    f_ssem,
    f_rsem,
    g_ssem,
    g_rsem,
    m_ssem,
    m_rsem,
    p_ssem,
    p_rsem,
    t_ssem,
    t_rsem,
):
    me = lax.axis_index("var")
    limit = count_ref[0]
    live_rows = limit - me * SENSORS

    def remote(src, dst, ssem, rsem, peer):
        return pltpu.make_async_remote_copy(
            src_ref=src,
            dst_ref=dst,
            send_sem=ssem,
            recv_sem=rsem,
            device_id={"var": peer},
            device_id_type=MESH,
        )

    loads = [
        pltpu.make_async_copy(src, dst, load_sems.at[i])
        for i, (src, dst) in enumerate(
            (
                (upstream_hbm, upstream),
                (series_hbm, series),
                (taps_hbm, taps),
                (up1_hbm, up1),
                (down1_hbm, down1),
                (down2_hbm, down2),
                (up2_hbm, up2),
            )
        )
    ]
    for load in loads:
        load.start()

    barrier = pltpu.get_barrier_semaphore()

    @pl.loop(1, PEERS)
    def _(o):
        pl.semaphore_signal(
            barrier, inc=1, device_id={"var": offset_peer(me, o, 1)}, device_id_type=MESH
        )

    loads[0].wait()
    row_index = lax.broadcasted_iota(jnp.int32, (SENSORS, PATCHES), 0)
    live_sensor = (row_index < live_rows).astype(F32)

    @pl.loop(0, SENSORS)
    def _(m):
        rows32[pl.ds(m, CHANNELS, stride=SENSORS), :] = upstream[m].astype(F32)

    @pl.loop(0, CHANNELS)
    def _(d):
        at = pl.multiple_of(d * SENSORS, SENSORS)
        u_send[d] = (rows32[pl.ds(at, SENSORS), :] * live_sensor).astype(BF16)

    pl.semaphore_wait(barrier, PEERS - 1)
    mine = pl.ds(pl.multiple_of(me * SENSORS, SENSORS), SENSORS)

    def u_copy(o, peer):
        return remote(
            u_send.at[pl.ds(OWN * peer, OWN)],
            u_recv.at[:, mine, :],
            u_ssem.at[o],
            u_rsem.at[o],
            peer,
        )

    @pl.loop(1, PEERS)
    def _(o):
        u_copy(o, offset_peer(me, o, 1)).start()

    u_self = pltpu.make_async_copy(
        u_send.at[pl.ds(OWN * me, OWN)], u_recv.at[:, mine, :], self_sems.at[0]
    )
    u_self.start()

    df1 = df1_ref[...].astype(F32)
    zero8 = jnp.zeros((8, CHANNELS), F32)
    dft[...] = jnp.concatenate(
        [
            jnp.concatenate([df1, zero8], axis=1),
            jnp.concatenate([zero8, df1], axis=1),
            jnp.zeros((112, 128), F32),
        ],
        axis=0,
    ).astype(BF16)
    uf1_32 = uf1_ref[...].astype(F32)
    ufr[0] = jnp.concatenate([uf1_32, jnp.zeros((120, HIDDEN), F32)], axis=0).astype(BF16)
    ufr[1] = jnp.concatenate(
        [jnp.zeros((8, HIDDEN), F32), uf1_32, jnp.zeros((112, HIDDEN), F32)], axis=0
    ).astype(BF16)

    loads[1].wait()
    loads[2].wait()
    padded[:, 0 : HALF * 8, :] = jnp.zeros((GROUPS, HALF * 8, 128), F32)
    padded[:, (HALF + PATCHES) * 8 : PADDED * 8, :] = jnp.zeros((GROUPS, HALF * 8, 128), F32)

    for g in range(GROUPS):

        @pl.loop(0, 8)
        def _(r):
            both = jnp.concatenate(
                [series[16 * g + r].astype(F32), series[16 * g + 8 + r].astype(F32)], axis=0
            )
            padded[g, pl.ds(HALF * 8 + r, PATCHES, stride=8), :] = both.T

    @pl.loop(0, TAPS)
    def _(k):
        row = taps[k].astype(F32)
        for g in range(GROUPS):
            packed_taps[k, g] = jnp.concatenate(
                [row[16 * g : 16 * g + 8], row[16 * g + 8 : 16 * g + 16]], axis=1
            )

    sub = lax.broadcasted_iota(jnp.int32, (8, 128), 0)
    lane = lax.broadcasted_iota(jnp.int32, (8, 128), 1)
    high = (lane >= CHANNELS).astype(jnp.int32) * 8

    def group_mask(g):
        return (sub + high + 16 * g < live_rows).astype(F32)

    def conv_group(g, sums):
        def conv_block(nb, acc_sum):
            base = pl.multiple_of(nb * (BLOCK * 8), BLOCK * 8)
            acc = [None] * BLOCK
            tap = {}
            for j in range(BLOCK + TAPS - 1):
                x = padded[g, pl.ds(base + 8 * j, 8), :]
                if j < TAPS:
                    tap[j] = packed_taps[j, g]
                for i in range(max(0, j - TAPS + 1), min(BLOCK - 1, j) + 1):
                    term = tap[j - i] * x
                    acc[i] = term if acc[i] is None else acc[i] + term
            for i in range(BLOCK):
                conv[g, pl.ds(base + 8 * i, 8), :] = acc[i]
                acc_sum = acc_sum + acc[i]
            return acc_sum

        group_sum = lax.fori_loop(0, PATCHES // BLOCK, conv_block, jnp.zeros((8, 128), F32))
        return sums + group_sum * group_mask(g)

    sums = lax.fori_loop(0, GROUPS, conv_group, jnp.zeros((8, 128), F32))

    def fold(v):
        v = jnp.sum(v, axis=0, keepdims=True)
        return v + pltpu.roll(v, CHANNELS, axis=1)

    sum_row = fold(sums)
    own_count = jnp.clip(live_rows, 0, SENSORS).astype(F32) * PATCHES
    own_mean = sum_row / jnp.maximum(own_count, 1.0)

    def square_group(g, squares):
        def block(b, acc):
            at = pl.multiple_of(b * 128, 128)
            c = conv[g, pl.ds(at, 128), :] - own_mean
            return acc + jnp.sum((c * c).reshape(16, 8, 128), axis=0)

        group = lax.fori_loop(0, 8, block, jnp.zeros((8, 128), F32))
        return squares + group * group_mask(g)

    square_row = fold(lax.fori_loop(0, GROUPS, square_group, jnp.zeros((8, 128), F32)))
    stats = jnp.where(
        sub == 0,
        sum_row,
        jnp.where(sub == 1, square_row, jnp.where(sub == 2, own_mean, own_count)),
    )
    st_send[...] = stats
    st_recv[me] = stats

    def st_copy(o, peer):
        return remote(st_send, st_recv.at[me], st_ssem.at[o], st_rsem.at[o], peer)

    @pl.loop(1, PEERS)
    def _(o):
        st_copy(o, offset_peer(me, o, 1)).start()

    @pl.loop(1, PEERS)
    def _(o):
        st_copy(o, offset_peer(me, o, 1)).wait()

    st_all = st_recv[...]
    st_sum = jnp.sum(st_all, axis=0)
    live_total = limit.astype(F32) * PATCHES
    bn_mean = st_sum[0:1] / live_total
    means = st_all[:, 2:3, :] - bn_mean[None]
    shift_squares = jnp.sum(st_all[:, 3:4, :] * means * means, axis=0)
    spread = (st_sum[1:2] + shift_squares) / live_total
    gain = jnp.concatenate([gain_ref[...], gain_ref[...]], axis=1)
    bias = jnp.concatenate([bias_ref[...], bias_ref[...]], axis=1)
    bn_scale = gain * lax.rsqrt(spread + 1e-05)

    loads[3].wait()
    loads[4].wait()
    zero_half = jnp.zeros((CHANNELS, HIDDEN), BF16)
    lane_row = lax.broadcasted_iota(jnp.int32, (1, 128), 1)
    high_row = (lane_row >= CHANNELS).astype(jnp.int32) * 8

    def f_copy(c, o, peer):
        return remote(
            f_send.at[c, pl.ds(OWN * peer, OWN)],
            f_recv.at[:, pl.ds(pl.multiple_of(me * SENSORS + c * CHUNK, CHUNK), CHUNK), :],
            f_ssem.at[c * PEERS + o],
            f_rsem.at[c * PEERS + o],
            peer,
        )

    f_self = []
    for c in range(CHUNKS):
        for gl in range(GROUPS // CHUNKS):
            g = c * (GROUPS // CHUNKS) + gl

            @pl.loop(0, 8)
            def _(r):
                pair = g * 8 + r
                live = (high_row + 16 * g + r < live_rows).astype(F32)
                centered = conv[g, pl.ds(r, PATCHES, stride=8), :] - bn_mean
                normed = ((centered * bn_scale + bias) * live).astype(BF16)
                normed_ref[pair] = normed
                low = dot(normed, dft[...], NT).astype(BF16)
                low_t[pair] = dot(dft[0:16, :], normed, NT).astype(BF16)
                lhs = jnp.concatenate([normed, low], axis=1)
                for half in range(2):
                    m = 16 * g + 8 * half + r
                    weight = up1[m]
                    rhs = jnp.concatenate(
                        [weight, zero_half, ufr[half]] if half == 0 else [zero_half, weight, ufr[half]],
                        axis=0,
                    )
                    value, slope = gelu_parts(dot(lhs, rhs))
                    slope_ref[m] = slope
                    feature = dot(down1[m], value.astype(BF16), NT)
                    rows32[pl.ds(16 * gl + 8 * half + r, CHANNELS, stride=CHUNK), :] = feature

        @pl.loop(0, CHANNELS)
        def _(d):
            at = pl.multiple_of(d * CHUNK, CHUNK)
            f_send[c, d] = rows32[pl.ds(at, CHUNK), :].astype(BF16)

        @pl.loop(1, PEERS)
        def _(o):
            f_copy(c, o, offset_peer(me, o, 1)).start()

        f_self.append(
            pltpu.make_async_copy(
                f_send.at[c, pl.ds(OWN * me, OWN)],
                f_recv.at[:, pl.ds(pl.multiple_of(me * SENSORS + c * CHUNK, CHUNK), CHUNK), :],
                self_sems.at[1 + c],
            )
        )
        f_self[-1].start()

    u_self.wait()

    @pl.loop(1, PEERS)
    def _(o):
        u_copy(o, offset_peer(me, o, 1)).wait()

    loads[5].wait()
    loads[6].wait()
    for dd in range(OWN):
        gh_ref[dd] = dot(down2[dd], u_recv[dd]).T

    for c in range(CHUNKS):
        f_self[c].wait()

        @pl.loop(1, PEERS)
        def _(o):
            f_copy(c, o, offset_peer(me, o, 1)).wait()

    for dd in range(OWN):

        def mix(b, carry):
            pre, low = carry
            at = pl.ds(pl.multiple_of(b * 256, 256), 256)
            f = f_recv[dd, at, :]
            return pre + dot(f, up2[dd, at, :], TN), low + dot(df2_ref[:, at], f)

        pre, low = lax.fori_loop(
            0,
            SLOTS // 256,
            mix,
            (jnp.zeros((PATCHES, HIDDEN), F32), jnp.zeros((8, PATCHES), F32)),
        )
        low = low.astype(BF16)
        value, slope = gelu_parts(pre + dot(low, uf2_ref[...], TN))
        hid_ref[dd] = value.astype(BF16)
        gp2 = (gh_ref[dd] * slope).astype(BF16)
        gp2_ref[dd] = gp2
        back_ref[dd] = dot(uf2_ref[...], gp2, NT).astype(BF16)
        gu2 = dot(low, gp2)
        for t in range(2):
            tile = gu2[:, 128 * t : 128 * (t + 1)]
            part[16 + t] = tile if dd == 0 else part[16 + t] + tile

    own_block = pl.ds(OWN * me, OWN)

    def g_copy(peer):
        o = offset_of(me, peer)
        return remote(g_send.at[peer], g_recv.at[own_block], g_ssem.at[o], g_rsem.at[o], peer)

    def m_copy(peer):
        o = offset_of(me, peer)
        return remote(m_send.at[peer], m_recv.at[own_block], m_ssem.at[o], m_rsem.at[o], peer)

    def send_both(copy, sender, receiver, sem, chip):
        for core in range(2):
            peer = 2 * chip + core

            @pl.when(peer != me)
            def _():
                copy(peer).start()

            @pl.when(peer == me)
            def _():
                pltpu.make_async_copy(sender.at[peer], receiver.at[own_block], sem).start()

    @pl.loop(1, 17)
    def _(i):
        chip = offset_peer(me, 2 * (i % 16), 1) // 2
        at = pl.ds(pl.multiple_of(chip * 128, 128), 128)
        gd2 = jnp.zeros((8, 128), F32)
        for dd in range(OWN):
            grad = dot(up2[dd, at, :], gp2_ref[dd], NT) + dot(df2_ref[:, at], back_ref[dd], TN)
            gd2 = gd2 + dot(back_ref[dd], f_recv[dd, at, :], NT)
            grad = grad.astype(BF16)
            g_send[2 * chip, dd] = grad[0:SENSORS]
            g_send[2 * chip + 1, dd] = grad[SENSORS:]
        part[chip] = gd2
        send_both(g_copy, g_send, g_recv, self_sems.at[3], chip)

    @pl.loop(1, 17)
    def _(i):
        chip = offset_peer(me, 2 * (i % 16), 1) // 2
        at = pl.ds(pl.multiple_of(chip * 128, 128), 128)
        for dd in range(OWN):
            mix_t = dot(hid_ref[dd], down2[dd, :, at]).T.astype(BF16)
            m_send[2 * chip, dd] = mix_t[0:SENSORS]
            m_send[2 * chip + 1, dd] = mix_t[SENSORS:]
        send_both(m_copy, m_send, m_recv, self_sems.at[4], chip)

    def self_wait(sender, receiver, sem):
        pltpu.make_async_copy(sender.at[me], receiver.at[own_block], sem).wait()

    self_wait(g_send, g_recv, self_sems.at[3])

    @pl.loop(1, PEERS)
    def _(o):
        g_copy(offset_peer(me, o, 1)).wait()

    @pl.loop(0, CHANNELS)
    def _(d):
        at = pl.multiple_of(d * SENSORS, SENSORS)
        rows32[pl.ds(at, SENSORS), :] = g_recv[d].astype(F32)

    gu1 = jnp.zeros((8, HIDDEN), F32)
    gd1 = jnp.zeros((16, 128), F32)
    for g in range(GROUPS):

        def back(r, carry):
            gu1, gd1 = carry
            pair = g * 8 + r
            grad = jnp.concatenate(
                [
                    rows32[pl.ds(16 * g + 8 * half + r, CHANNELS, stride=SENSORS), :]
                    for half in range(2)
                ],
                axis=0,
            ).T.astype(BF16)
            gps, backs = [], []
            for half in range(2):
                m = 16 * g + 8 * half + r
                weight = down1[m]
                rhs = jnp.concatenate(
                    [weight, zero_half] if half == 0 else [zero_half, weight], axis=0
                )
                gp = (dot(grad, rhs) * slope_ref[m]).astype(BF16)
                gps.append(gp)
                backs.append(dot(uf1_ref[...], gp, NT))
            low = low_t[pair].astype(F32)
            lhs = jnp.concatenate([low[0:8], low[8:16]], axis=1).astype(BF16)
            gu1 = gu1 + dot(lhs, jnp.concatenate(gps, axis=0))
            gd1 = gd1 + dot(jnp.concatenate(backs, axis=0).astype(BF16), normed_ref[pair])
            return gu1, gd1

        gu1, gd1 = lax.fori_loop(0, 8, back, (gu1, gd1))

    part[18] = gu1[:, 0:128]
    part[19] = gu1[:, 128:256]
    part[20] = jnp.where(lane < CHANNELS, gd1[0:8], gd1[8:16])

    TILES = 21
    part_recv[me] = part[jnp.minimum(me, TILES - 1)]

    def p_copy(tile, o):
        return remote(part.at[tile], part_recv.at[me], p_ssem.at[o], p_rsem.at[o], tile)

    @pl.loop(1, PEERS)
    def _(o):
        peer = offset_peer(me, o, 1)

        @pl.when(peer < TILES)
        def _():
            p_copy(peer, o).start()

    def t_copy(peer, o):
        return remote(total, total_recv.at[me], t_ssem.at[o], t_rsem.at[o], peer)

    @pl.when(me < TILES)
    def _():
        @pl.loop(1, PEERS)
        def _(o):
            p_copy(me, o).wait_recv()

        summed = jnp.sum(part_recv[...], axis=0)
        total[...] = summed
        total_recv[me] = summed

        @pl.loop(1, PEERS)
        def _(o):
            t_copy(offset_peer(me, o, 1), o).start()

    @pl.loop(1, PEERS)
    def _(o):
        source = offset_peer(me, o, -1)

        @pl.when(source < TILES)
        def _():
            t_copy(source, o).wait_recv()

    for t in range(16):
        gd2_ref[:, 128 * t : 128 * (t + 1)] = total_recv[t]
    for t in range(2):
        gu2_ref[:, 128 * t : 128 * (t + 1)] = total_recv[16 + t]
        gu1_ref[:, 128 * t : 128 * (t + 1)] = total_recv[18 + t]
    both = total_recv[20]
    gd1_ref[...] = (both + pltpu.roll(both, CHANNELS, axis=1))[:, 0:CHANNELS]

    self_wait(m_send, m_recv, self_sems.at[4])

    @pl.loop(1, PEERS)
    def _(o):
        m_copy(offset_peer(me, o, 1)).wait()

    @pl.loop(0, CHANNELS)
    def _(d):
        at = pl.multiple_of(d * SENSORS, SENSORS)
        rows32[pl.ds(at, SENSORS), :] = m_recv[d].astype(F32) * live_sensor

    @pl.loop(0, SENSORS)
    def _(m):
        out_buf[m] = (
            series[m].astype(F32) + rows32[pl.ds(m, CHANNELS, stride=SENSORS), :]
        ).astype(BF16)

    store = pltpu.make_async_copy(out_buf, mixed_hbm, load_sems.at[0])
    store.start()

    @pl.loop(1, PEERS)
    def _(o):
        peer = offset_peer(me, o, 1)

        @pl.when(peer < TILES)
        def _():
            p_copy(peer, o).wait_send()

        @pl.when(me < TILES)
        def _():
            t_copy(peer, o).wait_send()

    store.wait()


def body(
    series,
    sensor_total_count,
    depthwise_weight,
    batchnorm_gain,
    batchnorm_bias,
    channel_up_weight,
    channel_down_weight,
    down_factor1,
    up_factor1,
    sensor_up_weight,
    sensor_down_weight,
    down_factor2,
    up_factor2,
    upstream,
):
    vmem = pl.BlockSpec(memory_space=pltpu.VMEM)
    hbm = pl.BlockSpec(memory_space=pltpu.HBM)
    rows = PATCHES * 8
    dma = pltpu.SemaphoreType.DMA
    mixed, gd1, gu1, gd2, gu2 = pl.pallas_call(
        kernel,
        out_shape=(
            jax.ShapeDtypeStruct((SENSORS, CHANNELS, PATCHES), BF16),
            jax.ShapeDtypeStruct((8, CHANNELS), F32),
            jax.ShapeDtypeStruct((8, HIDDEN), F32),
            jax.ShapeDtypeStruct((8, SLOTS), F32),
            jax.ShapeDtypeStruct((8, HIDDEN), F32),
        ),
        in_specs=[pl.BlockSpec(memory_space=pltpu.SMEM)] + [vmem] * 6 + [hbm] * 7,
        out_specs=(hbm, vmem, vmem, vmem, vmem),
        scratch_shapes=[
            pltpu.VMEM((SENSORS, CHANNELS, PATCHES), BF16),
            pltpu.VMEM((TAPS, SENSORS, CHANNELS), BF16),
            pltpu.VMEM((SENSORS, CHANNELS, HIDDEN), BF16),
            pltpu.VMEM((SENSORS, CHANNELS, HIDDEN), BF16),
            pltpu.VMEM((OWN, SLOTS, HIDDEN), BF16),
            pltpu.VMEM((OWN, HIDDEN, SLOTS), BF16),
            pltpu.VMEM((SENSORS, CHANNELS, PATCHES), BF16),
            pltpu.VMEM((GROUPS, PADDED * 8, 128), F32),
            pltpu.VMEM((TAPS, GROUPS, 8, 128), F32),
            pltpu.VMEM((GROUPS, rows, 128), F32),
            pltpu.VMEM((SENSORS * CHANNELS, PATCHES), F32),
            pltpu.VMEM((SENSORS // 2, PATCHES, 128), BF16),
            pltpu.VMEM((SENSORS // 2, 16, PATCHES), BF16),
            pltpu.VMEM((SENSORS, PATCHES, HIDDEN), F32),
            pltpu.VMEM((CHANNELS, SENSORS, PATCHES), BF16),
            pltpu.VMEM((OWN, SLOTS, PATCHES), BF16),
            pltpu.VMEM((CHUNKS, CHANNELS, CHUNK, PATCHES), BF16),
            pltpu.VMEM((OWN, SLOTS, PATCHES), BF16),
            pltpu.VMEM((PEERS, OWN, SENSORS, PATCHES), BF16),
            pltpu.VMEM((CHANNELS, SENSORS, PATCHES), BF16),
            pltpu.VMEM((PEERS, OWN, SENSORS, PATCHES), BF16),
            pltpu.VMEM((CHANNELS, SENSORS, PATCHES), BF16),
            pltpu.VMEM((SENSORS, CHANNELS, PATCHES), BF16),
            pltpu.VMEM((8, 128), F32),
            pltpu.VMEM((PEERS, 8, 128), F32),
            pltpu.VMEM((128, 128), BF16),
            pltpu.VMEM((2, 128, HIDDEN), BF16),
            pltpu.VMEM((OWN, PATCHES, HIDDEN), F32),
            pltpu.VMEM((OWN, PATCHES, HIDDEN), BF16),
            pltpu.VMEM((OWN, PATCHES, HIDDEN), BF16),
            pltpu.VMEM((OWN, 8, PATCHES), BF16),
            pltpu.VMEM((PEERS, 8, 128), F32),
            pltpu.VMEM((PEERS, 8, 128), F32),
            pltpu.VMEM((8, 128), F32),
            pltpu.VMEM((PEERS, 8, 128), F32),
            dma((7,)),
            dma((5,)),
            dma((PEERS,)),
            dma((PEERS,)),
            dma((PEERS,)),
            dma((PEERS,)),
            dma((CHUNKS * PEERS,)),
            dma((CHUNKS * PEERS,)),
            dma((PEERS,)),
            dma((PEERS,)),
            dma((PEERS,)),
            dma((PEERS,)),
            dma((PEERS,)),
            dma((PEERS,)),
            dma((PEERS,)),
            dma((PEERS,)),
        ],
        compiler_params=pltpu.CompilerParams(
            collective_id=0, has_side_effects=True, vmem_limit_bytes=60 * 1024 * 1024
        ),
        cost_estimate=pl.CostEstimate(
            flops=2_000_000_000, bytes_accessed=12_000_000, transcendentals=2_200_000
        ),
    )(
        sensor_total_count,
        batchnorm_gain.reshape(1, CHANNELS),
        batchnorm_bias.reshape(1, CHANNELS),
        down_factor1.T,
        up_factor1,
        down_factor2.T,
        up_factor2,
        series[0],
        jnp.transpose(depthwise_weight, (2, 0, 1)),
        channel_up_weight,
        jnp.transpose(channel_down_weight, (0, 2, 1)),
        sensor_up_weight,
        sensor_down_weight,
        upstream[0],
    )
    return mixed[None], gd1.T, gu1, gd2.T, gu2


def solution(mesh):
    placed = (
        P("grp", "var", None, None),
        P("grp"),
        P("var", None, None),
        P(),
        P(),
        P("var", None, None),
        P("var", None, None),
        P(),
        P(),
        P("var", None, None),
        P("var", None, None),
        P(),
        P(),
        P("grp", "var", None, None),
    )
    return jax.shard_map(
        body,
        mesh=mesh,
        in_specs=placed,
        out_specs=(
            P("grp", "var", None, None),
            P("grp", None),
            P("grp", None),
            P("grp", None),
            P("grp", None),
        ),
        check_vma=False,
    )
```

time: 343 us -> 127 us (0.37); the launches traced: 338 us -> 127 us
  blocking collectives: 183 us -> 0 us
  Pallas kernels: 0 us -> 121 us
  matrix products: 43.4 us -> 0 us
  local copies, waits for them, and re-layouts: 40.1 us -> 4.73 us
  waiting for transfers between devices: 27.4 us -> 0 us
  starting transfers between devices: 26.6 us -> 0 us
  other arithmetic: 15.5 us -> 0 us
    psum x2 -> x0, blocking collectives: 183 us -> none  [the longest x1 120 us: body(): lax.psum(part_a1.astype(jnp.bfloat16), 'var').astype(jnp.float32)]
    pallas_call x0 -> x1, Pallas kernels: none -> 121 us  [body(): pl.pallas_call(kernel, out_shape=(jax.ShapeDtypeStruct((SENSORS, CHANNELS...]
    all_to_all x4 -> x0, waiting for transfers between devices: 27.4 us -> none  [the longest x1 11.2 us: body(): lax.all_to_all(grad_feat, 'var', split_axis=1, concat_axis=2, tiled=True)]
    dot_general x17 -> x0, matrix products: 27.1 us -> none  [the longest x1 8.02 us: body(): jnp.einsum('zyof,ylo->zylf', backward_gradient, channel_down_weight, pref...]
    all_to_all x4 -> x0, starting transfers between devices: 26.6 us -> none  [the longest x1 8.93 us: body(): lax.all_to_all(input_rows, 'var', split_axis=2, concat_axis=1, tiled=True)]
    conv_general_dilated x1 -> x0, matrix products: 16.3 us -> none  [depthwise(): lax.conv_general_dilated(stacked, kernel, (1,), [(tap_count // 2, tap_cou...]
    convert_element_type x9 -> x0, other arithmetic: 11.8 us -> none  [the longest x2 9.01 us: body(): normalized_rows = (shifted * live_mask).astype(jnp.bfloat16)]
    convert_element_type x4 -> x0, local copies, waits for them, and re-layouts: 9.22 us -> none  [the longest x1 3.67 us: mixing_forward(): mixed_two = jnp.einsum('bdnj,djm->bmdn', hidden_two, sensor_down_weight,...]
  transfers between devices with their start and end apart: 4 -> 0, of which waited for: 3 -> 0; matrix products, arithmetic and copies ran while one was open for 20% -> 0% of each run, Pallas kernels for 0% -> 0%
where the time goes in v1:
time: 127 us
  Pallas kernels  121 us (95%)
  local copies, waits for them, and re-layouts  4.73 us (4%)
  between operations  1.33 us (1%)
    pallas_call x1, Pallas kernels, body(): pl.pallas_call(kernel, out_shape=(jax.ShapeDtypeStruct((SENSORS, CHANNELS...  121 us
    unnamed x13, local copies, waits for them, and re-layouts  4.73 us

profile of v1, /device:TPU:1, one launch (start us, length us, event | category | flops | bytes accessed | tf_op | source)
XLA Modules:
  0.0 127.3 jit_solution(8833021497833902218)
XLA Ops:
  1.3 121.2 %shard_map.173 = (bf16[64,64,128]{2,1,0:T(8,128)(2,1)}, f32[8,64]{1,0:T(8,128)}, f32[8,256]{1,0:T(8,128)}, f32[8,2048]{1,0:T(8,128)}, f32[8,256]{1,0:T(8,128)}) custom-call(s32[1]{0:T(128)S(6)} %copy.24.count_ref, f32[1,64]{1,0:T(1,128)} %bitcast.20, f32[1,64]{1,0:T(1,128)} %bitcast.21, bf16[8,64]{1,0:T(8,128)(2,1)} %bitcast.19, bf16[8,256]{1,0:T(8,128)(2,1)} %uf1_ref.1, ...), custom_call_target="tpu_custom_call" | custom-call | flops 2000000000 | bytes 12000000 | tf_op jit(solution)/shard_map/pallas_call | solution.py:625
  122.5 0.0 copy-start.3
  122.5 0.0 copy-start.2
  122.5 0.0 copy-start
  122.5 0.0 copy-start.1
  122.5 2.3 %copy.25 = bf16[1,64,64,128]{3,2,1,0:T(8,128)(2,1)} copy(bf16[1,64,64,128]{3,2,1,0:T(8,128)(2,1)} %bitcast.14) | data formatting | bytes 2097152
  124.8 0.0 copy-done.3
  124.8 0.6 copy.26
  125.4 0.0 copy-done.2
  125.4 0.6 copy.27
  126.0 0.0 copy-done
  126.0 0.6 copy.28
  126.7 0.0 copy-done.1
  126.7 0.6 copy.29
Async XLA Ops:
  122.5 2.3 %copy-start.3 = (f32[8,64]{1,0:T(8,128)S(1)}, f32[8,64]{1,0:T(8,128)}, u32[]{:S(2)}) copy-start(f32[8,64]{1,0:T(8,128)} %get-tuple-element.11) | copy-start | bytes 6148
  122.5 2.9 %copy-start.2 = (f32[8,256]{1,0:T(8,128)S(1)}, f32[8,256]{1,0:T(8,128)}, u32[]{:S(2)}) copy-start(f32[8,256]{1,0:T(8,128)} %get-tuple-element.22) | copy-start | bytes 24580
  122.5 3.5 %copy-start = (f32[8,2048]{1,0:T(8,128)S(1)}, f32[8,2048]{1,0:T(8,128)}, u32[]{:S(2)}) copy-start(f32[8,2048]{1,0:T(8,128)} %get-tuple-element.13) | copy-start | bytes 196612
  122.5 4.1 %copy-start.1 = (f32[8,256]{1,0:T(8,128)S(1)}, f32[8,256]{1,0:T(8,128)}, u32[]{:S(2)}) copy-start(f32[8,256]{1,0:T(8,128)} %get-tuple-element.24) | copy-start | bytes 24580

commit v2 on v1

--- a/solution.py
+++ b/solution.py
@@ -23,8 +23,12 @@
 SLOTS = PEERS * SENSORS
 HIDDEN = 256
 OWN = 2
-CHUNKS = 2
+CHUNKS = 4
 CHUNK = SENSORS // CHUNKS
+HALVES = 2
+BATCH = SENSORS // HALVES
+TILES = 21
+STEP = 16
 BLOCK = 16
 
 
@@ -54,11 +58,8 @@
     )
 
 
-def offset_of(me, peer):
-    dx = (peer // 8 + 4 - me // 8) % 4
-    dy = ((peer // 2) % 4 + 4 - (me // 2) % 4) % 4
-    dc = (peer % 2 + 2 - me % 2) % 2
-    return dx * 8 + dy * 2 + dc
+def peer_at(me, i):
+    return offset_peer(me, (i + 18) % (PEERS - 1) + 1, 1)
 
 
 def kernel(
@@ -76,11 +77,8 @@
     up2_hbm,
     down2_hbm,
     upstream_hbm,
-    mixed_hbm,
-    gd1_ref,
-    gu1_ref,
-    gd2_ref,
-    gu2_ref,
+    m_recv,
+    total_out,
     series,
     taps,
     up1,
@@ -102,8 +100,6 @@
     g_send,
     g_recv,
     m_send,
-    m_recv,
-    out_buf,
     st_send,
     st_recv,
     dft,
@@ -118,20 +114,8 @@
     total_recv,
     load_sems,
     self_sems,
-    u_ssem,
-    u_rsem,
-    st_ssem,
-    st_rsem,
-    f_ssem,
-    f_rsem,
-    g_ssem,
-    g_rsem,
-    m_ssem,
-    m_rsem,
-    p_ssem,
-    p_rsem,
-    t_ssem,
-    t_rsem,
+    sends,
+    arrivals,
 ):
     me = lax.axis_index("var")
     limit = count_ref[0]
@@ -176,11 +160,11 @@
     row_index = lax.broadcasted_iota(jnp.int32, (SENSORS, PATCHES), 0)
     live_sensor = (row_index < live_rows).astype(F32)
 
-    @pl.loop(0, SENSORS)
+    @pl.loop(0, SENSORS, unroll=8)
     def _(m):
         rows32[pl.ds(m, CHANNELS, stride=SENSORS), :] = upstream[m].astype(F32)
 
-    @pl.loop(0, CHANNELS)
+    @pl.loop(0, CHANNELS, unroll=8)
     def _(d):
         at = pl.multiple_of(d * SENSORS, SENSORS)
         u_send[d] = (rows32[pl.ds(at, SENSORS), :] * live_sensor).astype(BF16)
@@ -188,23 +172,26 @@
     pl.semaphore_wait(barrier, PEERS - 1)
     mine = pl.ds(pl.multiple_of(me * SENSORS, SENSORS), SENSORS)
 
-    def u_copy(o, peer):
-        return remote(
-            u_send.at[pl.ds(OWN * peer, OWN)],
-            u_recv.at[:, mine, :],
-            u_ssem.at[o],
-            u_rsem.at[o],
-            peer,
-        )
+    neighbour = offset_peer(me, 1, 1)
 
     @pl.loop(1, PEERS)
-    def _(o):
-        u_copy(o, offset_peer(me, o, 1)).start()
+    def _(i):
+        peer = peer_at(me, i)
+        remote(
+            u_send.at[pl.ds(OWN * peer, OWN)], u_recv.at[:, mine, :], sends.at[0], arrivals.at[0], peer
+        ).start()
 
     u_self = pltpu.make_async_copy(
         u_send.at[pl.ds(OWN * me, OWN)], u_recv.at[:, mine, :], self_sems.at[0]
     )
     u_self.start()
+    u_all = remote(
+        u_send.at[pl.ds(0, OWN * (PEERS - 1))],
+        u_recv.at[:, pl.ds(0, SENSORS * (PEERS - 1)), :],
+        sends.at[0],
+        arrivals.at[0],
+        neighbour,
+    )
 
     df1 = df1_ref[...].astype(F32)
     zero8 = jnp.zeros((8, CHANNELS), F32)
@@ -229,14 +216,14 @@
 
     for g in range(GROUPS):
 
-        @pl.loop(0, 8)
+        @pl.loop(0, 8, unroll=4)
         def _(r):
             both = jnp.concatenate(
                 [series[16 * g + r].astype(F32), series[16 * g + 8 + r].astype(F32)], axis=0
             )
             padded[g, pl.ds(HALF * 8 + r, PATCHES, stride=8), :] = both.T
 
-    @pl.loop(0, TAPS)
+    @pl.loop(0, TAPS, unroll=3)
     def _(k):
         row = taps[k].astype(F32)
         for g in range(GROUPS):
@@ -299,17 +286,18 @@
     st_send[...] = stats
     st_recv[me] = stats
 
-    def st_copy(o, peer):
-        return remote(st_send, st_recv.at[me], st_ssem.at[o], st_rsem.at[o], peer)
-
     @pl.loop(1, PEERS)
-    def _(o):
-        st_copy(o, offset_peer(me, o, 1)).start()
-
-    @pl.loop(1, PEERS)
-    def _(o):
-        st_copy(o, offset_peer(me, o, 1)).wait()
-
+    def _(i):
+        remote(st_send, st_recv.at[me], sends.at[1], arrivals.at[1], peer_at(me, i)).start()
+
+    st_many = remote(
+        st_recv.at[pl.ds(0, PEERS - 1)],
+        st_recv.at[pl.ds(0, PEERS - 1)],
+        sends.at[1],
+        arrivals.at[1],
+        neighbour,
+    )
+    st_many.wait_recv()
     st_all = st_recv[...]
     st_sum = jnp.sum(st_all, axis=0)
     live_total = limit.astype(F32) * PATCHES
@@ -327,21 +315,31 @@
     lane_row = lax.broadcasted_iota(jnp.int32, (1, 128), 1)
     high_row = (lane_row >= CHANNELS).astype(jnp.int32) * 8
 
-    def f_copy(c, o, peer):
+    def f_copy(c, peer):
         return remote(
             f_send.at[c, pl.ds(OWN * peer, OWN)],
             f_recv.at[:, pl.ds(pl.multiple_of(me * SENSORS + c * CHUNK, CHUNK), CHUNK), :],
-            f_ssem.at[c * PEERS + o],
-            f_rsem.at[c * PEERS + o],
+            sends.at[2 + c],
+            arrivals.at[2 + c],
             peer,
         )
 
+    f_all = [
+        remote(
+            f_send.at[c, pl.ds(0, OWN * (PEERS - 1))],
+            f_recv.at[:, pl.ds(0, CHUNK * (PEERS - 1)), :],
+            sends.at[2 + c],
+            arrivals.at[2 + c],
+            neighbour,
+        )
+        for c in range(CHUNKS)
+    ]
     f_self = []
     for c in range(CHUNKS):
         for gl in range(GROUPS // CHUNKS):
             g = c * (GROUPS // CHUNKS) + gl
 
-            @pl.loop(0, 8)
+            @pl.loop(0, 8, unroll=4)
             def _(r):
                 pair = g * 8 + r
                 live = (high_row + 16 * g + r < live_rows).astype(F32)
@@ -363,14 +361,14 @@
                     feature = dot(down1[m], value.astype(BF16), NT)
                     rows32[pl.ds(16 * gl + 8 * half + r, CHANNELS, stride=CHUNK), :] = feature
 
-        @pl.loop(0, CHANNELS)
+        @pl.loop(0, CHANNELS, unroll=8)
         def _(d):
             at = pl.multiple_of(d * CHUNK, CHUNK)
             f_send[c, d] = rows32[pl.ds(at, CHUNK), :].astype(BF16)
 
         @pl.loop(1, PEERS)
-        def _(o):
-            f_copy(c, o, offset_peer(me, o, 1)).start()
+        def _(i):
+            f_copy(c, peer_at(me, i)).start()
 
         f_self.append(
             pltpu.make_async_copy(
@@ -382,10 +380,7 @@
         f_self[-1].start()
 
     u_self.wait()
-
-    @pl.loop(1, PEERS)
-    def _(o):
-        u_copy(o, offset_peer(me, o, 1)).wait()
+    u_all.wait_recv()
 
     loads[5].wait()
     loads[6].wait()
@@ -394,10 +389,7 @@
 
     for c in range(CHUNKS):
         f_self[c].wait()
-
-        @pl.loop(1, PEERS)
-        def _(o):
-            f_copy(c, o, offset_peer(me, o, 1)).wait()
+        f_all[c].wait_recv()
 
     for dd in range(OWN):
 
@@ -412,6 +404,7 @@
             SLOTS // 256,
             mix,
             (jnp.zeros((PATCHES, HIDDEN), F32), jnp.zeros((8, PATCHES), F32)),
+            unroll=2,
         )
         low = low.astype(BF16)
         value, slope = gelu_parts(pre + dot(low, uf2_ref[...], TN))
@@ -426,74 +419,112 @@
 
     own_block = pl.ds(OWN * me, OWN)
 
-    def g_copy(peer):
-        o = offset_of(me, peer)
-        return remote(g_send.at[peer], g_recv.at[own_block], g_ssem.at[o], g_rsem.at[o], peer)
+    def g_copy(half, peer):
+        return remote(
+            g_send.at[half, peer],
+            g_recv.at[half, own_block],
+            sends.at[6 + half],
+            arrivals.at[6 + half],
+            peer,
+        )
 
     def m_copy(peer):
-        o = offset_of(me, peer)
-        return remote(m_send.at[peer], m_recv.at[own_block], m_ssem.at[o], m_rsem.at[o], peer)
-
-    def send_both(copy, sender, receiver, sem, chip):
-        for core in range(2):
-            peer = 2 * chip + core
-
-            @pl.when(peer != me)
-            def _():
-                copy(peer).start()
-
-            @pl.when(peer == me)
-            def _():
-                pltpu.make_async_copy(sender.at[peer], receiver.at[own_block], sem).start()
-
-    @pl.loop(1, 17)
-    def _(i):
-        chip = offset_peer(me, 2 * (i % 16), 1) // 2
-        at = pl.ds(pl.multiple_of(chip * 128, 128), 128)
-        gd2 = jnp.zeros((8, 128), F32)
-        for dd in range(OWN):
-            grad = dot(up2[dd, at, :], gp2_ref[dd], NT) + dot(df2_ref[:, at], back_ref[dd], TN)
-            gd2 = gd2 + dot(back_ref[dd], f_recv[dd, at, :], NT)
-            grad = grad.astype(BF16)
-            g_send[2 * chip, dd] = grad[0:SENSORS]
-            g_send[2 * chip + 1, dd] = grad[SENSORS:]
-        part[chip] = gd2
-        send_both(g_copy, g_send, g_recv, self_sems.at[3], chip)
-
-    @pl.loop(1, 17)
-    def _(i):
-        chip = offset_peer(me, 2 * (i % 16), 1) // 2
-        at = pl.ds(pl.multiple_of(chip * 128, 128), 128)
-        for dd in range(OWN):
-            mix_t = dot(hid_ref[dd], down2[dd, :, at]).T.astype(BF16)
-            m_send[2 * chip, dd] = mix_t[0:SENSORS]
-            m_send[2 * chip + 1, dd] = mix_t[SENSORS:]
-        send_both(m_copy, m_send, m_recv, self_sems.at[4], chip)
-
-    def self_wait(sender, receiver, sem):
-        pltpu.make_async_copy(sender.at[me], receiver.at[own_block], sem).wait()
-
-    self_wait(g_send, g_recv, self_sems.at[3])
-
-    @pl.loop(1, PEERS)
-    def _(o):
-        g_copy(offset_peer(me, o, 1)).wait()
-
-    @pl.loop(0, CHANNELS)
-    def _(d):
-        at = pl.multiple_of(d * SENSORS, SENSORS)
-        rows32[pl.ds(at, SENSORS), :] = g_recv[d].astype(F32)
+        return remote(m_send.at[peer], m_recv.at[own_block], sends.at[8], arrivals.at[8], peer)
+
+    g_all = [
+        remote(
+            g_send.at[half, pl.ds(0, PEERS - 1)],
+            g_send.at[half, pl.ds(0, PEERS - 1)],
+            sends.at[6 + half],
+            arrivals.at[6 + half],
+            neighbour,
+        )
+        for half in range(HALVES)
+    ]
+    m_all = remote(
+        m_send.at[pl.ds(0, PEERS - 1)],
+        m_send.at[pl.ds(0, PEERS - 1)],
+        sends.at[8],
+        arrivals.at[8],
+        neighbour,
+    )
+    g_self = [
+        pltpu.make_async_copy(
+            g_send.at[half, me], g_recv.at[half, own_block], self_sems.at[5 + half]
+        )
+        for half in range(HALVES)
+    ]
+    m_self = pltpu.make_async_copy(m_send.at[me], m_recv.at[own_block], self_sems.at[7])
+
+    def to_chips(copy, first):
+        for i in range(4):
+            for core in range(2):
+                peer = 2 * chip_at(first + i) + core
+
+                @pl.when(peer != me)
+                def _():
+                    copy(peer).start()
+
+    def chip_at(i):
+        return offset_peer(me, 2 * ((i + 10) % 16), 1) // 2
+
+    @pl.loop(0, 4)
+    def _(q):
+        for i in range(4):
+            chip = chip_at(4 * q + i)
+            at = pl.ds(pl.multiple_of(chip * 128, 128), 128)
+            gd2 = []
+            for dd in range(OWN):
+                grad = dot(up2[dd, at, :], gp2_ref[dd], NT) + dot(
+                    df2_ref[:, at], back_ref[dd], TN
+                )
+                gd2.append(dot(back_ref[dd], f_recv[dd, at, :], NT))
+                grad = grad.astype(BF16)
+                for part_of in range(4):
+                    core, half = part_of // 2, part_of % 2
+                    g_send[half, 2 * chip + core, dd] = grad[BATCH * part_of : BATCH * (part_of + 1)]
+            part[chip] = gd2[0] + gd2[1]
+        to_chips(lambda peer: g_copy(0, peer), 4 * q)
+
+    @pl.loop(0, 4)
+    def _(q):
+        to_chips(lambda peer: g_copy(1, peer), 4 * q)
+
+    for half in range(HALVES):
+        g_self[half].start()
+
+    @pl.loop(0, 4)
+    def _(q):
+        for i in range(4):
+            chip = chip_at(4 * q + i)
+            at = pl.ds(pl.multiple_of(chip * 128, 128), 128)
+            for dd in range(OWN):
+                mix_t = dot(hid_ref[dd], down2[dd, :, at]).T.astype(BF16)
+                m_send[2 * chip, dd] = mix_t[0:SENSORS]
+                m_send[2 * chip + 1, dd] = mix_t[SENSORS:]
+        to_chips(m_copy, 4 * q)
+
+    m_self.start()
 
     gu1 = jnp.zeros((8, HIDDEN), F32)
     gd1 = jnp.zeros((16, 128), F32)
     for g in range(GROUPS):
+        half_of = g // 2
+        if g % 2 == 0:
+            g_self[half_of].wait()
+            g_all[half_of].wait_recv()
+
+            @pl.loop(0, CHANNELS, unroll=8)
+            def _(d):
+                at = pl.multiple_of(d * BATCH, BATCH)
+                rows32[pl.ds(at, BATCH), :] = g_recv[half_of, d].astype(F32)
 
         def back(r, carry):
             gu1, gd1 = carry
             pair = g * 8 + r
             grad = jnp.concatenate(
                 [
-                    rows32[pl.ds(16 * g + 8 * half + r, CHANNELS, stride=SENSORS), :]
+                    rows32[pl.ds(16 * (g % 2) + 8 * half + r, CHANNELS, stride=BATCH), :]
                     for half in range(2)
                 ],
                 axis=0,
@@ -514,92 +545,91 @@
             gd1 = gd1 + dot(jnp.concatenate(backs, axis=0).astype(BF16), normed_ref[pair])
             return gu1, gd1
 
-        gu1, gd1 = lax.fori_loop(0, 8, back, (gu1, gd1))
+        gu1, gd1 = lax.fori_loop(0, 8, back, (gu1, gd1), unroll=4)
 
     part[18] = gu1[:, 0:128]
     part[19] = gu1[:, 128:256]
     part[20] = jnp.where(lane < CHANNELS, gd1[0:8], gd1[8:16])
 
-    TILES = 21
     part_recv[me] = part[jnp.minimum(me, TILES - 1)]
 
-    def p_copy(tile, o):
-        return remote(part.at[tile], part_recv.at[me], p_ssem.at[o], p_rsem.at[o], tile)
-
     @pl.loop(1, PEERS)
-    def _(o):
-        peer = offset_peer(me, o, 1)
+    def _(i):
+        peer = peer_at(me, i)
 
         @pl.when(peer < TILES)
         def _():
-            p_copy(peer, o).start()
-
-    def t_copy(peer, o):
-        return remote(total, total_recv.at[me], t_ssem.at[o], t_rsem.at[o], peer)
+            remote(part.at[peer], part_recv.at[me], sends.at[9], arrivals.at[9], peer).start()
+
+    def tiles(n, ref, at):
+        return remote(
+            ref.at[pl.ds(0, n)], ref.at[pl.ds(0, n)], sends.at[at], arrivals.at[at], neighbour
+        )
 
     @pl.when(me < TILES)
     def _():
-        @pl.loop(1, PEERS)
-        def _(o):
-            p_copy(me, o).wait_recv()
-
+        tiles(PEERS - 1, part_recv, 9).wait_recv()
         summed = jnp.sum(part_recv[...], axis=0)
         total[...] = summed
         total_recv[me] = summed
 
         @pl.loop(1, PEERS)
-        def _(o):
-            t_copy(offset_peer(me, o, 1), o).start()
-
-    @pl.loop(1, PEERS)
-    def _(o):
-        source = offset_peer(me, o, -1)
-
-        @pl.when(source < TILES)
-        def _():
-            t_copy(source, o).wait_recv()
-
-    for t in range(16):
-        gd2_ref[:, 128 * t : 128 * (t + 1)] = total_recv[t]
-    for t in range(2):
-        gu2_ref[:, 128 * t : 128 * (t + 1)] = total_recv[16 + t]
-        gu1_ref[:, 128 * t : 128 * (t + 1)] = total_recv[18 + t]
-    both = total_recv[20]
-    gd1_ref[...] = (both + pltpu.roll(both, CHANNELS, axis=1))[:, 0:CHANNELS]
-
-    self_wait(m_send, m_recv, self_sems.at[4])
-
-    @pl.loop(1, PEERS)
-    def _(o):
-        m_copy(offset_peer(me, o, 1)).wait()
-
-    @pl.loop(0, CHANNELS)
+        def _(i):
+            remote(
+                total, total_recv.at[me], sends.at[10], arrivals.at[10], peer_at(me, i)
+            ).start()
+
+        tiles(TILES - 1, total_recv, 10).wait_recv()
+
+    @pl.when(me >= TILES)
+    def _():
+        tiles(TILES, total_recv, 10).wait_recv()
+
+    total_out[...] = total_recv[0:TILES]
+
+    m_self.wait()
+    m_all.wait_recv()
+    u_all.wait_send()
+    st_many.wait_send()
+    for sent in f_all + g_all + [m_all]:
+        sent.wait_send()
+
+    @pl.when(me < TILES)
+    def _():
+        tiles(TILES - 1, part, 9).wait_send()
+        tiles(PEERS - 1, total_recv, 10).wait_send()
+
+    @pl.when(me >= TILES)
+    def _():
+        tiles(TILES, part, 9).wait_send()
+
+
+def finish(
+    count_ref, series, received, total, mixed, gd1_ref, gu1_ref, gd2_ref, gu2_ref, rows32
+):
+    step = pl.program_id(0)
+    row = lax.broadcasted_iota(jnp.int32, (STEP, PATCHES), 0) + step * STEP
+    live = (row < count_ref[0] - lax.axis_index("var") * SENSORS).astype(F32)
+
+    @pl.loop(0, CHANNELS, unroll=16)
     def _(d):
-        at = pl.multiple_of(d * SENSORS, SENSORS)
-        rows32[pl.ds(at, SENSORS), :] = m_recv[d].astype(F32) * live_sensor
-
-    @pl.loop(0, SENSORS)
+        rows32[pl.ds(pl.multiple_of(d * STEP, STEP), STEP), :] = received[d].astype(F32) * live
+
+    @pl.loop(0, STEP, unroll=4)
     def _(m):
-        out_buf[m] = (
-            series[m].astype(F32) + rows32[pl.ds(m, CHANNELS, stride=SENSORS), :]
+        mixed[m] = (
+            series[m].astype(F32) + rows32[pl.ds(m, CHANNELS, stride=STEP), :]
         ).astype(BF16)
 
-    store = pltpu.make_async_copy(out_buf, mixed_hbm, load_sems.at[0])
-    store.start()
-
-    @pl.loop(1, PEERS)
-    def _(o):
-        peer = offset_peer(me, o, 1)
-
-        @pl.when(peer < TILES)
-        def _():
-            p_copy(peer, o).wait_send()
-
-        @pl.when(me < TILES)
-        def _():
-            t_copy(peer, o).wait_send()
-
-    store.wait()
+    @pl.when(step == 0)
+    def _():
+        for t in range(16):
+            gd2_ref[:, 128 * t : 128 * (t + 1)] = total[t]
+        for t in range(2):
+            gu2_ref[:, 128 * t : 128 * (t + 1)] = total[16 + t]
+            gu1_ref[:, 128 * t : 128 * (t + 1)] = total[18 + t]
+        both = total[20]
+        gd1_ref[...] = (both + pltpu.roll(both, CHANNELS, axis=1))[:, 0:CHANNELS]
 
 
 def body(
@@ -622,17 +652,14 @@
     hbm = pl.BlockSpec(memory_space=pltpu.HBM)
     rows = PATCHES * 8
     dma = pltpu.SemaphoreType.DMA
-    mixed, gd1, gu1, gd2, gu2 = pl.pallas_call(
+    received, total = pl.pallas_call(
         kernel,
         out_shape=(
-            jax.ShapeDtypeStruct((SENSORS, CHANNELS, PATCHES), BF16),
-            jax.ShapeDtypeStruct((8, CHANNELS), F32),
-            jax.ShapeDtypeStruct((8, HIDDEN), F32),
-            jax.ShapeDtypeStruct((8, SLOTS), F32),
-            jax.ShapeDtypeStruct((8, HIDDEN), F32),
+            jax.ShapeDtypeStruct((CHANNELS, SENSORS, PATCHES), BF16),
+            jax.ShapeDtypeStruct((TILES, 8, 128), F32),
         ),
         in_specs=[pl.BlockSpec(memory_space=pltpu.SMEM)] + [vmem] * 6 + [hbm] * 7,
-        out_specs=(hbm, vmem, vmem, vmem, vmem),
+        out_specs=(hbm, vmem),
         scratch_shapes=[
             pltpu.VMEM((SENSORS, CHANNELS, PATCHES), BF16),
             pltpu.VMEM((TAPS, SENSORS, CHANNELS), BF16),
@@ -652,11 +679,9 @@
             pltpu.VMEM((OWN, SLOTS, PATCHES), BF16),
             pltpu.VMEM((CHUNKS, CHANNELS, CHUNK, PATCHES), BF16),
             pltpu.VMEM((OWN, SLOTS, PATCHES), BF16),
+            pltpu.VMEM((HALVES, PEERS, OWN, BATCH, PATCHES), BF16),
+            pltpu.VMEM((HALVES, CHANNELS, BATCH, PATCHES), BF16),
             pltpu.VMEM((PEERS, OWN, SENSORS, PATCHES), BF16),
-            pltpu.VMEM((CHANNELS, SENSORS, PATCHES), BF16),
-            pltpu.VMEM((PEERS, OWN, SENSORS, PATCHES), BF16),
-            pltpu.VMEM((CHANNELS, SENSORS, PATCHES), BF16),
-            pltpu.VMEM((SENSORS, CHANNELS, PATCHES), BF16),
             pltpu.VMEM((8, 128), F32),
             pltpu.VMEM((PEERS, 8, 128), F32),
             pltpu.VMEM((128, 128), BF16),
@@ -670,21 +695,9 @@
             pltpu.VMEM((8, 128), F32),
             pltpu.VMEM((PEERS, 8, 128), F32),
             dma((7,)),
-            dma((5,)),
-            dma((PEERS,)),
-            dma((PEERS,)),
-            dma((PEERS,)),
-            dma((PEERS,)),
-            dma((CHUNKS * PEERS,)),
-            dma((CHUNKS * PEERS,)),
-            dma((PEERS,)),
-            dma((PEERS,)),
-            dma((PEERS,)),
-            dma((PEERS,)),
-            dma((PEERS,)),
-            dma((PEERS,)),
-            dma((PEERS,)),
-            dma((PEERS,)),
+            dma((8,)),
+            dma((11,)),
+            dma((11,)),
         ],
         compiler_params=pltpu.CompilerParams(
             collective_id=0, has_side_effects=True, vmem_limit_bytes=60 * 1024 * 1024
@@ -708,6 +721,34 @@
         sensor_down_weight,
         upstream[0],
     )
+    whole = lambda *shape: pl.BlockSpec(shape, lambda i: (0,) * len(shape))
+    sensors_block = pl.BlockSpec((STEP, CHANNELS, PATCHES), lambda i: (i, 0, 0))
+    mixed, gd1, gu1, gd2, gu2 = pl.pallas_call(
+        finish,
+        out_shape=(
+            jax.ShapeDtypeStruct((SENSORS, CHANNELS, PATCHES), BF16),
+            jax.ShapeDtypeStruct((8, CHANNELS), F32),
+            jax.ShapeDtypeStruct((8, HIDDEN), F32),
+            jax.ShapeDtypeStruct((8, SLOTS), F32),
+            jax.ShapeDtypeStruct((8, HIDDEN), F32),
+        ),
+        grid=(SENSORS // STEP,),
+        in_specs=[
+            pl.BlockSpec(memory_space=pltpu.SMEM),
+            sensors_block,
+            pl.BlockSpec((CHANNELS, STEP, PATCHES), lambda i: (0, i, 0)),
+            whole(TILES, 8, 128),
+        ],
+        out_specs=(
+            sensors_block,
+            whole(8, CHANNELS),
+            whole(8, HIDDEN),
+            whole(8, SLOTS),
+            whole(8, HIDDEN),
+        ),
+        scratch_shapes=[pltpu.VMEM((STEP * CHANNELS, PATCHES), F32)],
+        compiler_params=pltpu.CompilerParams(vmem_limit_bytes=32 * 1024 * 1024),
+    )(sensor_total_count, series[0], received, total)
     return mixed[None], gd1.T, gu1, gd2.T, gu2
 
 

time: 127 us -> 91.7 us (0.72)
  Pallas kernels: 121 us -> 88.1 us
  local copies, waits for them, and re-layouts: 4.73 us -> 2.11 us
    pallas_call x1 -> x2, Pallas kernels: 121 us -> 88.1 us  [the longest x1 85.6 us: body(): pl.pallas_call(kernel, out_shape=(jax.ShapeDtypeStruct((CHANNELS, SENSORS...]
    unnamed x13 -> x6, local copies, waits for them, and re-layouts: 4.73 us -> 2.11 us
where the time goes in v2:
time: 91.7 us; the launch traced here: 91.5 us
  Pallas kernels  88.1 us (96%)
  local copies, waits for them, and re-layouts  2.11 us (2%)
  between operations  1.32 us (1%)
    pallas_call x1, Pallas kernels, body(): pl.pallas_call(kernel, out_shape=(jax.ShapeDtypeStruct((CHANNELS, SENSORS...  85.6 us
    pallas_call x1, Pallas kernels, body(): pl.pallas_call(finish, out_shape=(jax.ShapeDtypeStruct((SENSORS, CHANNELS...  2.44 us
    unnamed x6, local copies, waits for them, and re-layouts  2.11 us

profile of v2, /device:TPU:1, one launch (start us, length us, event | category | flops | bytes accessed | tf_op | source)
XLA Modules:
  0.0 91.5 jit_solution(459778814949550045)
XLA Ops:
  1.3 0.0 copy-start
  1.3 85.6 %shard_map.173 = (bf16[64,64,128]{2,1,0:T(8,128)(2,1)}, f32[21,8,128]{2,1,0:T(8,128)}) custom-call(s32[1]{0:T(128)S(6)} %copy.19.count_ref, f32[1,64]{1,0:T(1,128)} %bitcast.18, f32[1,64]{1,0:T(1,128)} %bitcast.19, bf16[8,64]{1,0:T(8,128)(2,1)} %bitcast.17, bf16[8,256]{1,0:T(8,128)(2,1)} %uf1_ref.1, bf16[8,2048]{1,0:T(8,128)(2,1)} %bitcast.16, ...), custom_call_target="tpu_custom_call" | custom-call | flops 2000000000 | bytes 12000000 | tf_op jit(solution)/shard_map/pallas_call | solution.py:655
  86.9 0.0 copy-done
  86.9 0.0 copy-start.1
  86.9 1.2 %copy-done.1 = bf16[64,64,128]{2,1,0:T(8,128)(2,1)S(1)} copy-done((bf16[64,64,128]{2,1,0:T(8,128)(2,1)S(1)}, bf16[64,64,128]{2,1,0:T(8,128)(2,1)}, u32[]{:S(2)}) %copy-start.1) | copy-done | bytes 1048600
  88.2 0.0 copy-start.2
  88.2 0.9 copy-done.2
  89.0 2.4 %shard_map.174 = (bf16[64,64,128]{2,1,0:T(8,128)(2,1)}, f32[8,64]{1,0:T(8,128)}, f32[8,256]{1,0:T(8,128)}, f32[8,2048]{1,0:T(8,128)}, f32[8,256]{1,0:T(8,128)}) custom-call(s32[1]{0:T(128)S(6)} %copy.19.count_ref, bf16[64,64,128]{2,1,0:T(8,128)(2,1)S(1)} %bitcast.12, bf16[64,64,128]{2,1,0:T(8,128)(2,1)S(1)} %copy-done.1, f32[21,8,128]{2,1,0:T(8,128)S(1)} %copy-done.2), custom_call_target="tpu_custom_call" | custom-call | tf_op jit(solution)/shard_map/pallas_call | solution.py:726
Async XLA Ops:
  1.3 85.6 %copy-start = (bf16[1,64,64,128]{3,2,1,0:T(8,128)(2,1)S(1)}, bf16[1,64,64,128]{3,2,1,0:T(8,128)(2,1)}, u32[]{:S(2)}) copy-start(bf16[1,64,64,128]{3,2,1,0:T(8,128)(2,1)} %param.14) | copy-start | bytes 3145732
  86.9 1.2 %copy-start.1 = (bf16[64,64,128]{2,1,0:T(8,128)(2,1)S(1)}, bf16[64,64,128]{2,1,0:T(8,128)(2,1)}, u32[]{:S(2)}) copy-start(bf16[64,64,128]{2,1,0:T(8,128)(2,1)} %get-tuple-element.12.received) | copy-start | bytes 3145732
  88.2 0.9 copy-start.2

commit v3 on v2

--- a/solution.py
+++ b/solution.py
@@ -50,16 +50,12 @@
 TN = ((0,), (0,))
 
 
-def offset_peer(me, offset, sign):
-    x, y, c = me // 8, (me // 2) % 4, me % 2
-    dx, dy, dc = offset // 8, (offset // 2) % 4, offset % 2
-    return (
-        ((x + 4 + sign * dx) % 4) * 8 + ((y + 4 + sign * dy) % 4) * 2 + (c + 2 + sign * dc) % 2
-    )
-
-
-def peer_at(me, i):
-    return offset_peer(me, (i + 18) % (PEERS - 1) + 1, 1)
+def each_peer(me, act):
+    for first, last, unroll in ((16, PEERS, 4), (1, 16, 5)):
+
+        @pl.loop(first, last, unroll=unroll)
+        def _(i):
+            act(lax.rem(me + i, PEERS))
 
 
 def kernel(
@@ -150,11 +146,10 @@
 
     barrier = pltpu.get_barrier_semaphore()
 
-    @pl.loop(1, PEERS)
-    def _(o):
-        pl.semaphore_signal(
-            barrier, inc=1, device_id={"var": offset_peer(me, o, 1)}, device_id_type=MESH
-        )
+    def greet(peer):
+        pl.semaphore_signal(barrier, inc=1, device_id={"var": peer}, device_id_type=MESH)
+
+    each_peer(me, greet)
 
     loads[0].wait()
     row_index = lax.broadcasted_iota(jnp.int32, (SENSORS, PATCHES), 0)
@@ -168,30 +163,6 @@
     def _(d):
         at = pl.multiple_of(d * SENSORS, SENSORS)
         u_send[d] = (rows32[pl.ds(at, SENSORS), :] * live_sensor).astype(BF16)
-
-    pl.semaphore_wait(barrier, PEERS - 1)
-    mine = pl.ds(pl.multiple_of(me * SENSORS, SENSORS), SENSORS)
-
-    neighbour = offset_peer(me, 1, 1)
-
-    @pl.loop(1, PEERS)
-    def _(i):
-        peer = peer_at(me, i)
-        remote(
-            u_send.at[pl.ds(OWN * peer, OWN)], u_recv.at[:, mine, :], sends.at[0], arrivals.at[0], peer
-        ).start()
-
-    u_self = pltpu.make_async_copy(
-        u_send.at[pl.ds(OWN * me, OWN)], u_recv.at[:, mine, :], self_sems.at[0]
-    )
-    u_self.start()
-    u_all = remote(
-        u_send.at[pl.ds(0, OWN * (PEERS - 1))],
-        u_recv.at[:, pl.ds(0, SENSORS * (PEERS - 1)), :],
-        sends.at[0],
-        arrivals.at[0],
-        neighbour,
-    )
 
     df1 = df1_ref[...].astype(F32)
     zero8 = jnp.zeros((8, CHANNELS), F32)
@@ -216,7 +187,7 @@
 
     for g in range(GROUPS):
 
-        @pl.loop(0, 8, unroll=4)
+        @pl.loop(0, 8, unroll=8)
         def _(r):
             both = jnp.concatenate(
                 [series[16 * g + r].astype(F32), series[16 * g + 8 + r].astype(F32)], axis=0
@@ -230,6 +201,28 @@
             packed_taps[k, g] = jnp.concatenate(
                 [row[16 * g : 16 * g + 8], row[16 * g + 8 : 16 * g + 16]], axis=1
             )
+
+    pl.semaphore_wait(barrier, PEERS - 1)
+    mine = pl.ds(pl.multiple_of(me * SENSORS, SENSORS), SENSORS)
+    neighbour = lax.rem(me + 1, PEERS)
+
+    def u_start(peer):
+        remote(
+            u_send.at[pl.ds(OWN * peer, OWN)], u_recv.at[:, mine, :], sends.at[0], arrivals.at[0], peer
+        ).start()
+
+    each_peer(me, u_start)
+    u_self = pltpu.make_async_copy(
+        u_send.at[pl.ds(OWN * me, OWN)], u_recv.at[:, mine, :], self_sems.at[0]
+    )
+    u_self.start()
+    u_all = remote(
+        u_send.at[pl.ds(0, OWN * (PEERS - 1))],
+        u_recv.at[:, pl.ds(0, SENSORS * (PEERS - 1)), :],
+        sends.at[0],
+        arrivals.at[0],
+        neighbour,
+    )
 
     sub = lax.broadcasted_iota(jnp.int32, (8, 128), 0)
     lane = lax.broadcasted_iota(jnp.int32, (8, 128), 1)
@@ -286,9 +279,12 @@
     st_send[...] = stats
     st_recv[me] = stats
 
-    @pl.loop(1, PEERS)
-    def _(i):
-        remote(st_send, st_recv.at[me], sends.at[1], arrivals.at[1], peer_at(me, i)).start()
+    each_peer(
+        me,
+        lambda peer: remote(
+            st_send, st_recv.at[me], sends.at[1], arrivals.at[1], peer
+        ).start(),
+    )
 
     st_many = remote(
         st_recv.at[pl.ds(0, PEERS - 1)],
@@ -339,7 +335,7 @@
         for gl in range(GROUPS // CHUNKS):
             g = c * (GROUPS // CHUNKS) + gl
 
-            @pl.loop(0, 8, unroll=4)
+            @pl.loop(0, 8, unroll=8)
             def _(r):
                 pair = g * 8 + r
                 live = (high_row + 16 * g + r < live_rows).astype(F32)
@@ -366,9 +362,7 @@
             at = pl.multiple_of(d * CHUNK, CHUNK)
             f_send[c, d] = rows32[pl.ds(at, CHUNK), :].astype(BF16)
 
-        @pl.loop(1, PEERS)
-        def _(i):
-            f_copy(c, peer_at(me, i)).start()
+        each_peer(me, lambda peer: f_copy(c, peer).start())
 
         f_self.append(
             pltpu.make_async_copy(
@@ -456,60 +450,117 @@
     ]
     m_self = pltpu.make_async_copy(m_send.at[me], m_recv.at[own_block], self_sems.at[7])
 
-    def to_chips(copy, first):
-        for i in range(4):
-            for core in range(2):
-                peer = 2 * chip_at(first + i) + core
-
-                @pl.when(peer != me)
-                def _():
-                    copy(peer).start()
+    own_chip = me // 2
+    sibling = 2 * own_chip + 1 - lax.rem(me, 2)
 
     def chip_at(i):
-        return offset_peer(me, 2 * ((i + 10) % 16), 1) // 2
-
-    @pl.loop(0, 4)
-    def _(q):
-        for i in range(4):
-            chip = chip_at(4 * q + i)
-            at = pl.ds(pl.multiple_of(chip * 128, 128), 128)
-            gd2 = []
-            for dd in range(OWN):
-                grad = dot(up2[dd, at, :], gp2_ref[dd], NT) + dot(
-                    df2_ref[:, at], back_ref[dd], TN
-                )
-                gd2.append(dot(back_ref[dd], f_recv[dd, at, :], NT))
-                grad = grad.astype(BF16)
-                for part_of in range(4):
-                    core, half = part_of // 2, part_of % 2
-                    g_send[half, 2 * chip + core, dd] = grad[BATCH * part_of : BATCH * (part_of + 1)]
-            part[chip] = gd2[0] + gd2[1]
-        to_chips(lambda peer: g_copy(0, peer), 4 * q)
-
-    @pl.loop(0, 4)
-    def _(q):
-        to_chips(lambda peer: g_copy(1, peer), 4 * q)
-
+        return lax.rem(own_chip + 1 + lax.rem(i + 7, 15), 16)
+
+    def each_chip(act, send):
+        @pl.loop(0, 5)
+        def _(q):
+            chips = [chip_at(3 * q + i) for i in range(3)]
+            if act is not None:
+                for chip in chips:
+                    act(chip)
+            for chip in chips:
+                send(2 * chip)
+                send(2 * chip + 1)
+
+        if act is not None:
+            act(own_chip)
+        send(sibling)
+
+    def g_block(chip):
+        at = pl.ds(pl.multiple_of(chip * 128, 128), 128)
+        gd2 = []
+        for dd in range(OWN):
+            grad = dot(up2[dd, at, :], gp2_ref[dd], NT) + dot(df2_ref[:, at], back_ref[dd], TN)
+            gd2.append(dot(back_ref[dd], f_recv[dd, at, :], NT))
+            grad = grad.astype(BF16)
+            for part_of in range(4):
+                core, half = part_of // 2, part_of % 2
+                g_send[half, 2 * chip + core, dd] = grad[BATCH * part_of : BATCH * (part_of + 1)]
+        part[chip] = gd2[0] + gd2[1]
+
+    def m_block(chip):
+        at = pl.ds(pl.multiple_of(chip * 128, 128), 128)
+        for dd in range(OWN):
+            mix_t = dot(hid_ref[dd], down2[dd, :, at]).T.astype(BF16)
+            m_send[2 * chip, dd] = mix_t[0:SENSORS]
+            m_send[2 * chip + 1, dd] = mix_t[SENSORS:]
+
+    each_chip(g_block, lambda peer: g_copy(0, peer).start())
+    each_chip(None, lambda peer: g_copy(1, peer).start())
     for half in range(HALVES):
         g_self[half].start()
 
-    @pl.loop(0, 4)
-    def _(q):
-        for i in range(4):
-            chip = chip_at(4 * q + i)
-            at = pl.ds(pl.multiple_of(chip * 128, 128), 128)
-            for dd in range(OWN):
-                mix_t = dot(hid_ref[dd], down2[dd, :, at]).T.astype(BF16)
-                m_send[2 * chip, dd] = mix_t[0:SENSORS]
-                m_send[2 * chip + 1, dd] = mix_t[SENSORS:]
-        to_chips(m_copy, 4 * q)
-
+    def tiles(n, ref, at):
+        return remote(
+            ref.at[pl.ds(0, n)], ref.at[pl.ds(0, n)], sends.at[at], arrivals.at[at], neighbour
+        )
+
+    def is_owner(device, first, last):
+        return jnp.logical_and(device >= first, device < last)
+
+    def to_owners(first, last, at):
+        @pl.loop(first, last)
+        def _(owner):
+            @pl.when(owner != me)
+            def _():
+                remote(
+                    part.at[owner], part_recv.at[me], sends.at[at], arrivals.at[at], owner
+                ).start()
+
+        @pl.when(is_owner(me, first, last))
+        def _():
+            part_recv[me] = part[me]
+
+    def from_owners(first, last, at):
+        @pl.when(is_owner(me, first, last))
+        def _():
+            tiles(PEERS - 1, part_recv, at).wait_recv()
+            summed = jnp.sum(part_recv[...], axis=0)
+            total[...] = summed
+            total_recv[me] = summed
+            each_peer(
+                me,
+                lambda peer: remote(
+                    total, total_recv.at[me], sends.at[at + 1], arrivals.at[at + 1], peer
+                ).start(),
+            )
+
+    def by_role(first, last, owner_act, other_act):
+        owner = is_owner(me, first, last)
+        pl.when(owner)(owner_act)
+        pl.when(jnp.logical_not(owner))(other_act)
+
+    def totals_arrive(first, last, at):
+        by_role(
+            first,
+            last,
+            lambda: tiles(last - first - 1, total_recv, at + 1).wait_recv(),
+            lambda: tiles(last - first, total_recv, at + 1).wait_recv(),
+        )
+
+    def totals_left(first, last, at):
+        def owner_act():
+            tiles(last - first - 1, part, at).wait_send()
+            tiles(PEERS - 1, total_recv, at + 1).wait_send()
+
+        by_role(first, last, owner_act, lambda: tiles(last - first, part, at).wait_send())
+
+    to_owners(0, 18, 9)
+
+    each_chip(m_block, lambda peer: m_copy(peer).start())
     m_self.start()
 
     gu1 = jnp.zeros((8, HIDDEN), F32)
     gd1 = jnp.zeros((16, 128), F32)
     for g in range(GROUPS):
         half_of = g // 2
+        if g == 2:
+            from_owners(0, 18, 9)
         if g % 2 == 0:
             g_self[half_of].wait()
             g_all[half_of].wait_recv()
@@ -545,46 +596,16 @@
             gd1 = gd1 + dot(jnp.concatenate(backs, axis=0).astype(BF16), normed_ref[pair])
             return gu1, gd1
 
-        gu1, gd1 = lax.fori_loop(0, 8, back, (gu1, gd1), unroll=4)
+        gu1, gd1 = lax.fori_loop(0, 8, back, (gu1, gd1), unroll=8)
 
     part[18] = gu1[:, 0:128]
     part[19] = gu1[:, 128:256]
     part[20] = jnp.where(lane < CHANNELS, gd1[0:8], gd1[8:16])
 
-    part_recv[me] = part[jnp.minimum(me, TILES - 1)]
-
-    @pl.loop(1, PEERS)
-    def _(i):
-        peer = peer_at(me, i)
-
-        @pl.when(peer < TILES)
-        def _():
-            remote(part.at[peer], part_recv.at[me], sends.at[9], arrivals.at[9], peer).start()
-
-    def tiles(n, ref, at):
-        return remote(
-            ref.at[pl.ds(0, n)], ref.at[pl.ds(0, n)], sends.at[at], arrivals.at[at], neighbour
-        )
-
-    @pl.when(me < TILES)
-    def _():
-        tiles(PEERS - 1, part_recv, 9).wait_recv()
-        summed = jnp.sum(part_recv[...], axis=0)
-        total[...] = summed
-        total_recv[me] = summed
-
-        @pl.loop(1, PEERS)
-        def _(i):
-            remote(
-                total, total_recv.at[me], sends.at[10], arrivals.at[10], peer_at(me, i)
-            ).start()
-
-        tiles(TILES - 1, total_recv, 10).wait_recv()
-
-    @pl.when(me >= TILES)
-    def _():
-        tiles(TILES, total_recv, 10).wait_recv()
-
+    to_owners(18, TILES, 11)
+    from_owners(18, TILES, 11)
+    totals_arrive(0, 18, 9)
+    totals_arrive(18, TILES, 11)
     total_out[...] = total_recv[0:TILES]
 
     m_self.wait()
@@ -594,42 +615,84 @@
     for sent in f_all + g_all + [m_all]:
         sent.wait_send()
 
-    @pl.when(me < TILES)
-    def _():
-        tiles(TILES - 1, part, 9).wait_send()
-        tiles(PEERS - 1, total_recv, 10).wait_send()
-
-    @pl.when(me >= TILES)
-    def _():
-        tiles(TILES, part, 9).wait_send()
+    totals_left(0, 18, 9)
+    totals_left(18, TILES, 11)
 
 
 def finish(
-    count_ref, series, received, total, mixed, gd1_ref, gu1_ref, gd2_ref, gu2_ref, rows32
+    count_ref,
+    series_hbm,
+    received_hbm,
+    total_hbm,
+    mixed_hbm,
+    gd1_ref,
+    gu1_ref,
+    gd2_ref,
+    gu2_ref,
+    series,
+    received,
+    total,
+    mixed,
+    rows32,
+    load_sems,
+    store_sems,
 ):
-    step = pl.program_id(0)
-    row = lax.broadcasted_iota(jnp.int32, (STEP, PATCHES), 0) + step * STEP
-    live = (row < count_ref[0] - lax.axis_index("var") * SENSORS).astype(F32)
-
-    @pl.loop(0, CHANNELS, unroll=16)
-    def _(d):
-        rows32[pl.ds(pl.multiple_of(d * STEP, STEP), STEP), :] = received[d].astype(F32) * live
-
-    @pl.loop(0, STEP, unroll=4)
-    def _(m):
-        mixed[m] = (
-            series[m].astype(F32) + rows32[pl.ds(m, CHANNELS, stride=STEP), :]
-        ).astype(BF16)
-
-    @pl.when(step == 0)
-    def _():
-        for t in range(16):
-            gd2_ref[:, 128 * t : 128 * (t + 1)] = total[t]
-        for t in range(2):
-            gu2_ref[:, 128 * t : 128 * (t + 1)] = total[16 + t]
-            gu1_ref[:, 128 * t : 128 * (t + 1)] = total[18 + t]
-        both = total[20]
-        gd1_ref[...] = (both + pltpu.roll(both, CHANNELS, axis=1))[:, 0:CHANNELS]
+    steps = SENSORS // STEP
+    loads = [
+        pltpu.make_async_copy(
+            received_hbm.at[:, pl.ds(step * STEP, STEP), :], received.at[step], load_sems.at[step]
+        )
+        for step in range(steps)
+    ]
+    loads.append(pltpu.make_async_copy(total_hbm, total, load_sems.at[steps]))
+    blocks = [pl.ds(step * STEP, STEP) for step in range(steps)]
+    series_loads = [
+        pltpu.make_async_copy(
+            series_hbm.at[blocks[step]], series.at[blocks[step]], load_sems.at[steps + 1 + step]
+        )
+        for step in range(steps)
+    ]
+    for step in range(steps):
+        loads[step].start()
+        series_loads[step].start()
+    loads[steps].start()
+    live_rows = count_ref[0] - lax.axis_index("var") * SENSORS
+    row = lax.broadcasted_iota(jnp.int32, (STEP, PATCHES), 0)
+    stores = []
+    for step in range(steps):
+        loads[step].wait()
+        series_loads[step].wait()
+        live = (row + step * STEP < live_rows).astype(F32)
+
+        @pl.loop(0, CHANNELS, unroll=16)
+        def _(d):
+            rows32[pl.ds(pl.multiple_of(d * STEP, STEP), STEP), :] = (
+                received[step, d].astype(F32) * live
+            )
+
+        @pl.loop(0, STEP, unroll=8)
+        def _(m):
+            mixed[step * STEP + m] = (
+                series[step * STEP + m].astype(F32) + rows32[pl.ds(m, CHANNELS, stride=STEP), :]
+            ).astype(BF16)
+
+        stores.append(
+            pltpu.make_async_copy(
+                mixed.at[blocks[step]], mixed_hbm.at[blocks[step]], store_sems.at[step]
+            )
+        )
+        stores[-1].start()
+
+    loads[steps].wait()
+    for t in range(16):
+        gd2_ref[:, 128 * t : 128 * (t + 1)] = total[t]
+    for t in range(2):
+        gu2_ref[:, 128 * t : 128 * (t + 1)] = total[16 + t]
+        gu1_ref[:, 128 * t : 128 * (t + 1)] = total[18 + t]
+    both = total[20]
+    gd1_ref[...] = (both + pltpu.roll(both, CHANNELS, axis=1))[:, 0:CHANNELS]
+    for store in stores:
+        store.wait()
 
 
 def body(
@@ -696,8 +759,8 @@
             pltpu.VMEM((PEERS, 8, 128), F32),
             dma((7,)),
             dma((8,)),
-            dma((11,)),
-            dma((11,)),
+            dma((13,)),
+            dma((13,)),
         ],
         compiler_params=pltpu.CompilerParams(
             collective_id=0, has_side_effects=True, vmem_limit_bytes=60 * 1024 * 1024
@@ -721,8 +784,6 @@
         sensor_down_weight,
         upstream[0],
     )
-    whole = lambda *shape: pl.BlockSpec(shape, lambda i: (0,) * len(shape))
-    sensors_block = pl.BlockSpec((STEP, CHANNELS, PATCHES), lambda i: (i, 0, 0))
     mixed, gd1, gu1, gd2, gu2 = pl.pallas_call(
         finish,
         out_shape=(
@@ -732,22 +793,18 @@
             jax.ShapeDtypeStruct((8, SLOTS), F32),
             jax.ShapeDtypeStruct((8, HIDDEN), F32),
         ),
-        grid=(SENSORS // STEP,),
-        in_specs=[
-            pl.BlockSpec(memory_space=pltpu.SMEM),
-            sensors_block,
-            pl.BlockSpec((CHANNELS, STEP, PATCHES), lambda i: (0, i, 0)),
-            whole(TILES, 8, 128),
+        in_specs=[pl.BlockSpec(memory_space=pltpu.SMEM), hbm, hbm, hbm],
+        out_specs=(hbm, vmem, vmem, vmem, vmem),
+        scratch_shapes=[
+            pltpu.VMEM((SENSORS, CHANNELS, PATCHES), BF16),
+            pltpu.VMEM((SENSORS // STEP, CHANNELS, STEP, PATCHES), BF16),
+            pltpu.VMEM((TILES, 8, 128), F32),
+            pltpu.VMEM((SENSORS, CHANNELS, PATCHES), BF16),
+            pltpu.VMEM((STEP * CHANNELS, PATCHES), F32),
+            dma((2 * (SENSORS // STEP) + 1,)),
+            dma((SENSORS // STEP,)),
         ],
-        out_specs=(
-            sensors_block,
-            whole(8, CHANNELS),
-            whole(8, HIDDEN),
-            whole(8, SLOTS),
-            whole(8, HIDDEN),
-        ),
-        scratch_shapes=[pltpu.VMEM((STEP * CHANNELS, PATCHES), F32)],
-        compiler_params=pltpu.CompilerParams(vmem_limit_bytes=32 * 1024 * 1024),
+        compiler_params=pltpu.CompilerParams(vmem_limit_bytes=60 * 1024 * 1024),
     )(sensor_total_count, series[0], received, total)
     return mixed[None], gd1.T, gu1, gd2.T, gu2
 

time: 91.7 us -> 88.6 us (0.966)
  local copies, waits for them, and re-layouts: 2.11 us -> 0 us
  Pallas kernels: 88.1 us -> 87 us
    unnamed x6 -> x0, local copies, waits for them, and re-layouts: 2.11 us -> none
    pallas_call x1, Pallas kernels: 85.6 us -> 83.5 us  [body(): pl.pallas_call(kernel, out_shape=(jax.ShapeDtypeStruct((CHANNELS, SENSORS...]
    pallas_call x1, Pallas kernels: 2.44 us -> 3.43 us  [body(): pl.pallas_call(finish, out_shape=(jax.ShapeDtypeStruct((SENSORS, CHANNELS...]
where the time goes in v3:
time: 88.6 us; the launch traced here: 88.4 us
  Pallas kernels  87 us (98%)
  between operations  1.45 us (2%)
    pallas_call x1, Pallas kernels, body(): pl.pallas_call(kernel, out_shape=(jax.ShapeDtypeStruct((CHANNELS, SENSORS...  83.5 us
    pallas_call x1, Pallas kernels, body(): pl.pallas_call(finish, out_shape=(jax.ShapeDtypeStruct((SENSORS, CHANNELS...  3.43 us

profile of v3, /device:TPU:1, one launch (start us, length us, event | category | flops | bytes accessed | tf_op | source)
XLA Modules:
  0.0 88.4 jit_solution(14092653029582456659)
XLA Ops:
  1.3 83.5 %shard_map.173 = (bf16[64,64,128]{2,1,0:T(8,128)(2,1)}, f32[21,8,128]{2,1,0:T(8,128)}) custom-call(s32[1]{0:T(128)S(6)} %copy.19.count_ref, f32[1,64]{1,0:T(1,128)} %bitcast.18, f32[1,64]{1,0:T(1,128)} %bitcast.19, bf16[8,64]{1,0:T(8,128)(2,1)} %bitcast.17, bf16[8,256]{1,0:T(8,128)(2,1)} %uf1_ref.1, bf16[8,2048]{1,0:T(8,128)(2,1)} %bitcast.16, ...), custom_call_target="tpu_custom_call" | custom-call | flops 2000000000 | bytes 12000000 | tf_op jit(solution)/shard_map/pallas_call | solution.py:718
  84.8 3.4 %shard_map.174 = (bf16[64,64,128]{2,1,0:T(8,128)(2,1)}, f32[8,64]{1,0:T(8,128)}, f32[8,256]{1,0:T(8,128)}, f32[8,2048]{1,0:T(8,128)}, f32[8,256]{1,0:T(8,128)}) custom-call(s32[1]{0:T(128)S(6)} %copy.19.count_ref, bf16[64,64,128]{2,1,0:T(8,128)(2,1)} %bitcast.12, bf16[64,64,128]{2,1,0:T(8,128)(2,1)} %get-tuple-element.12.received_hbm, ...), custom_call_target="tpu_custom_call" | custom-call | tf_op jit(solution)/shard_map/pallas_call | solution.py:787

commit v4 on v3

--- a/solution.py
+++ b/solution.py
@@ -28,6 +28,8 @@
 HALVES = 2
 BATCH = SENSORS // HALVES
 TILES = 21
+FIRST_SENDS = 7
+ORDER = tuple(range(16, PEERS)) + tuple(range(1, 16))
 STEP = 16
 BLOCK = 16
 
@@ -141,7 +143,7 @@
             )
         )
     ]
-    for load in loads:
+    for load in loads[:3]:
         load.start()
 
     barrier = pltpu.get_barrier_semaphore()
@@ -182,6 +184,8 @@
 
     loads[1].wait()
     loads[2].wait()
+    for load in loads[3:]:
+        load.start()
     padded[:, 0 : HALF * 8, :] = jnp.zeros((GROUPS, HALF * 8, 128), F32)
     padded[:, (HALF + PATCHES) * 8 : PADDED * 8, :] = jnp.zeros((GROUPS, HALF * 8, 128), F32)
 
@@ -211,7 +215,8 @@
             u_send.at[pl.ds(OWN * peer, OWN)], u_recv.at[:, mine, :], sends.at[0], arrivals.at[0], peer
         ).start()
 
-    each_peer(me, u_start)
+    for offset in range(FIRST_SENDS):
+        u_start(lax.rem(me + PEERS - 1 - offset, PEERS))
     u_self = pltpu.make_async_copy(
         u_send.at[pl.ds(OWN * me, OWN)], u_recv.at[:, mine, :], self_sems.at[0]
     )
@@ -231,8 +236,10 @@
     def group_mask(g):
         return (sub + high + 16 * g < live_rows).astype(F32)
 
-    def conv_group(g, sums):
+    def conv_group(g, sums, sending=True):
         def conv_block(nb, acc_sum):
+            if sending:
+                u_start(lax.rem(me + 1 + 8 * g + nb, PEERS))
             base = pl.multiple_of(nb * (BLOCK * 8), BLOCK * 8)
             acc = [None] * BLOCK
             tap = {}
@@ -251,7 +258,8 @@
         group_sum = lax.fori_loop(0, PATCHES // BLOCK, conv_block, jnp.zeros((8, 128), F32))
         return sums + group_sum * group_mask(g)
 
-    sums = lax.fori_loop(0, GROUPS, conv_group, jnp.zeros((8, 128), F32))
+    sums = lax.fori_loop(0, GROUPS - 1, conv_group, jnp.zeros((8, 128), F32))
+    sums = conv_group(GROUPS - 1, sums, sending=False)
 
     def fold(v):
         v = jnp.sum(v, axis=0, keepdims=True)
@@ -332,37 +340,35 @@
     ]
     f_self = []
     for c in range(CHUNKS):
-        for gl in range(GROUPS // CHUNKS):
-            g = c * (GROUPS // CHUNKS) + gl
-
-            @pl.loop(0, 8, unroll=8)
-            def _(r):
-                pair = g * 8 + r
-                live = (high_row + 16 * g + r < live_rows).astype(F32)
-                centered = conv[g, pl.ds(r, PATCHES, stride=8), :] - bn_mean
-                normed = ((centered * bn_scale + bias) * live).astype(BF16)
-                normed_ref[pair] = normed
-                low = dot(normed, dft[...], NT).astype(BF16)
-                low_t[pair] = dot(dft[0:16, :], normed, NT).astype(BF16)
-                lhs = jnp.concatenate([normed, low], axis=1)
-                for half in range(2):
-                    m = 16 * g + 8 * half + r
-                    weight = up1[m]
-                    rhs = jnp.concatenate(
-                        [weight, zero_half, ufr[half]] if half == 0 else [zero_half, weight, ufr[half]],
-                        axis=0,
-                    )
-                    value, slope = gelu_parts(dot(lhs, rhs))
-                    slope_ref[m] = slope
-                    feature = dot(down1[m], value.astype(BF16), NT)
-                    rows32[pl.ds(16 * gl + 8 * half + r, CHANNELS, stride=CHUNK), :] = feature
-
-        @pl.loop(0, CHANNELS, unroll=8)
+        g = c
+        for r in range(8):
+            if c > 0:
+                for offset in ORDER[4 * r : 4 * r + 4]:
+                    f_copy(c - 1, lax.rem(me + offset, PEERS)).start()
+            pair = g * 8 + r
+            live = (high_row + 16 * g + r < live_rows).astype(F32)
+            centered = conv[g, pl.ds(r, PATCHES, stride=8), :] - bn_mean
+            normed = ((centered * bn_scale + bias) * live).astype(BF16)
+            normed_ref[pair] = normed
+            low = dot(normed, dft[...], NT).astype(BF16)
+            low_t[pair] = dot(dft[0:16, :], normed, NT).astype(BF16)
+            lhs = jnp.concatenate([normed, low], axis=1)
+            for half in range(2):
+                m = 16 * g + 8 * half + r
+                weight = up1[m]
+                rhs = jnp.concatenate(
+                    [weight, zero_half, ufr[half]] if half == 0 else [zero_half, weight, ufr[half]],
+                    axis=0,
+                )
+                value, slope = gelu_parts(dot(lhs, rhs))
+                slope_ref[m] = slope
+                feature = dot(down1[m], value.astype(BF16), NT)
+                rows32[pl.ds(8 * half + r, CHANNELS, stride=CHUNK), :] = feature
+
+        @pl.loop(0, CHANNELS, unroll=16)
         def _(d):
             at = pl.multiple_of(d * CHUNK, CHUNK)
             f_send[c, d] = rows32[pl.ds(at, CHUNK), :].astype(BF16)
-
-        each_peer(me, lambda peer: f_copy(c, peer).start())
 
         f_self.append(
             pltpu.make_async_copy(
@@ -372,6 +378,8 @@
             )
         )
         f_self[-1].start()
+
+    each_peer(me, lambda peer: f_copy(CHUNKS - 1, peer).start())
 
     u_self.wait()
     u_all.wait_recv()
@@ -456,20 +464,13 @@
     def chip_at(i):
         return lax.rem(own_chip + 1 + lax.rem(i + 7, 15), 16)
 
-    def each_chip(act, send):
-        @pl.loop(0, 5)
-        def _(q):
-            chips = [chip_at(3 * q + i) for i in range(3)]
-            if act is not None:
-                for chip in chips:
-                    act(chip)
-            for chip in chips:
-                send(2 * chip)
-                send(2 * chip + 1)
-
-        if act is not None:
-            act(own_chip)
-        send(sibling)
+    def trio(q):
+        return [chip_at(3 * q + i) for i in range(3)]
+
+    def to_trio(q, copy):
+        for chip in trio(q):
+            copy(2 * chip).start()
+            copy(2 * chip + 1).start()
 
     def g_block(chip):
         at = pl.ds(pl.multiple_of(chip * 128, 128), 128)
@@ -490,10 +491,37 @@
             m_send[2 * chip, dd] = mix_t[0:SENSORS]
             m_send[2 * chip + 1, dd] = mix_t[SENSORS:]
 
-    each_chip(g_block, lambda peer: g_copy(0, peer).start())
-    each_chip(None, lambda peer: g_copy(1, peer).start())
+    def g_first(peer):
+        return g_copy(0, peer)
+
+    def g_second(peer):
+        return g_copy(1, peer)
+
+    for chip in trio(0):
+        g_block(chip)
+
+    @pl.loop(1, 5)
+    def _(q):
+        to_trio(q - 1, g_first)
+        for chip in trio(q):
+            g_block(chip)
+
+    to_trio(4, g_first)
+    g_block(own_chip)
+    g_first(sibling).start()
     for half in range(HALVES):
         g_self[half].start()
+
+    @pl.loop(0, 5)
+    def _(q):
+        to_trio(q, g_second)
+        for chip in trio(q):
+            m_block(chip)
+
+    g_second(sibling).start()
+    m_block(own_chip)
+    each_peer(me, lambda peer: m_copy(peer).start())
+    m_self.start()
 
     def tiles(n, ref, at):
         return remote(
@@ -551,9 +579,6 @@
         by_role(first, last, owner_act, lambda: tiles(last - first, part, at).wait_send())
 
     to_owners(0, 18, 9)
-
-    each_chip(m_block, lambda peer: m_copy(peer).start())
-    m_self.start()
 
     gu1 = jnp.zeros((8, HIDDEN), F32)
     gd1 = jnp.zeros((16, 128), F32)

time: 88.6 us -> 103 us (1.16)
  Pallas kernels: 87 us -> 101 us
    pallas_call x1, Pallas kernels: 83.5 us -> 97.7 us  [body(): pl.pallas_call(kernel, out_shape=(jax.ShapeDtypeStruct((CHANNELS, SENSORS...]
where the time goes in v4:
time: 103 us
  Pallas kernels  101 us (98%)
  between operations  1.45 us (1%)
    pallas_call x1, Pallas kernels, body(): pl.pallas_call(kernel, out_shape=(jax.ShapeDtypeStruct((CHANNELS, SENSORS...  97.7 us
    pallas_call x1, Pallas kernels, body(): pl.pallas_call(finish, out_shape=(jax.ShapeDtypeStruct((SENSORS, CHANNELS...  3.43 us

profile of v4, /device:TPU:1, one launch (start us, length us, event | category | flops | bytes accessed | tf_op | source)
XLA Modules:
  0.0 102.6 jit_solution(5749504215649283437)
XLA Ops:
  1.3 97.7 %shard_map.173 = (bf16[64,64,128]{2,1,0:T(8,128)(2,1)}, f32[21,8,128]{2,1,0:T(8,128)}) custom-call(s32[1]{0:T(128)S(6)} %copy.19.count_ref, f32[1,64]{1,0:T(1,128)} %bitcast.18, f32[1,64]{1,0:T(1,128)} %bitcast.19, bf16[8,64]{1,0:T(8,128)(2,1)} %bitcast.17, bf16[8,256]{1,0:T(8,128)(2,1)} %uf1_ref.1, bf16[8,2048]{1,0:T(8,128)(2,1)} %bitcast.16, ...), custom_call_target="tpu_custom_call" | custom-call | flops 2000000000 | bytes 12000000 | tf_op jit(solution)/shard_map/pallas_call | solution.py:743
  99.0 3.4 %shard_map.174 = (bf16[64,64,128]{2,1,0:T(8,128)(2,1)}, f32[8,64]{1,0:T(8,128)}, f32[8,256]{1,0:T(8,128)}, f32[8,2048]{1,0:T(8,128)}, f32[8,256]{1,0:T(8,128)}) custom-call(s32[1]{0:T(128)S(6)} %copy.19.count_ref, bf16[64,64,128]{2,1,0:T(8,128)(2,1)} %bitcast.12, bf16[64,64,128]{2,1,0:T(8,128)(2,1)} %get-tuple-element.12.received_hbm, ...), custom_call_target="tpu_custom_call" | custom-call | tf_op jit(solution)/shard_map/pallas_call | solution.py:812

commit v5 on v3

--- a/solution.py
+++ b/solution.py
@@ -23,7 +23,7 @@
 SLOTS = PEERS * SENSORS
 HIDDEN = 256
 OWN = 2
-CHUNKS = 4
+CHUNKS = 2
 CHUNK = SENSORS // CHUNKS
 HALVES = 2
 BATCH = SENSORS // HALVES
@@ -141,7 +141,7 @@
             )
         )
     ]
-    for load in loads:
+    for load in loads[:3]:
         load.start()
 
     barrier = pltpu.get_barrier_semaphore()
@@ -182,6 +182,8 @@
 
     loads[1].wait()
     loads[2].wait()
+    for load in loads[3:]:
+        load.start()
     padded[:, 0 : HALF * 8, :] = jnp.zeros((GROUPS, HALF * 8, 128), F32)
     padded[:, (HALF + PATCHES) * 8 : PADDED * 8, :] = jnp.zeros((GROUPS, HALF * 8, 128), F32)
 
@@ -550,10 +552,9 @@
 
         by_role(first, last, owner_act, lambda: tiles(last - first, part, at).wait_send())
 
-    to_owners(0, 18, 9)
-
     each_chip(m_block, lambda peer: m_copy(peer).start())
     m_self.start()
+    to_owners(0, 18, 9)
 
     gu1 = jnp.zeros((8, HIDDEN), F32)
     gd1 = jnp.zeros((16, 128), F32)

time: 88.6 us -> 98 us (1.11)
  Pallas kernels: 87 us -> 96.4 us
    pallas_call x1, Pallas kernels: 83.5 us -> 92.9 us  [body(): pl.pallas_call(kernel, out_shape=(jax.ShapeDtypeStruct((CHANNELS, SENSORS...]
where the time goes in v5:
time: 98 us; the launch traced here: 97.8 us
  Pallas kernels  96.4 us (98%)
  between operations  1.45 us (1%)
    pallas_call x1, Pallas kernels, body(): pl.pallas_call(kernel, out_shape=(jax.ShapeDtypeStruct((CHANNELS, SENSORS...  92.9 us
    pallas_call x1, Pallas kernels, body(): pl.pallas_call(finish, out_shape=(jax.ShapeDtypeStruct((SENSORS, CHANNELS...  3.43 us

profile of v5, /device:TPU:1, one launch (start us, length us, event | category | flops | bytes accessed | tf_op | source)
XLA Modules:
  0.0 97.8 jit_solution(199487631738010427)
XLA Ops:
  1.3 92.9 %shard_map.173 = (bf16[64,64,128]{2,1,0:T(8,128)(2,1)}, f32[21,8,128]{2,1,0:T(8,128)}) custom-call(s32[1]{0:T(128)S(6)} %copy.19.count_ref, f32[1,64]{1,0:T(1,128)} %bitcast.18, f32[1,64]{1,0:T(1,128)} %bitcast.19, bf16[8,64]{1,0:T(8,128)(2,1)} %bitcast.17, bf16[8,256]{1,0:T(8,128)(2,1)} %uf1_ref.1, bf16[8,2048]{1,0:T(8,128)(2,1)} %bitcast.16, ...), custom_call_target="tpu_custom_call" | custom-call | flops 2000000000 | bytes 12000000 | tf_op jit(solution)/shard_map/pallas_call | solution.py:719
  94.2 3.4 %shard_map.174 = (bf16[64,64,128]{2,1,0:T(8,128)(2,1)}, f32[8,64]{1,0:T(8,128)}, f32[8,256]{1,0:T(8,128)}, f32[8,2048]{1,0:T(8,128)}, f32[8,256]{1,0:T(8,128)}) custom-call(s32[1]{0:T(128)S(6)} %copy.19.count_ref, bf16[64,64,128]{2,1,0:T(8,128)(2,1)} %bitcast.12, bf16[64,64,128]{2,1,0:T(8,128)(2,1)} %get-tuple-element.12.received_hbm, ...), custom_call_target="tpu_custom_call" | custom-call | tf_op jit(solution)/shard_map/pallas_call | solution.py:788

commit v6 on v3

--- a/solution.py
+++ b/solution.py
@@ -314,7 +314,7 @@
     def f_copy(c, peer):
         return remote(
             f_send.at[c, pl.ds(OWN * peer, OWN)],
-            f_recv.at[:, pl.ds(pl.multiple_of(me * SENSORS + c * CHUNK, CHUNK), CHUNK), :],
+            f_recv.at[:, me, pl.ds(c * CHUNK, CHUNK), :],
             sends.at[2 + c],
             arrivals.at[2 + c],
             peer,
@@ -323,7 +323,7 @@
     f_all = [
         remote(
             f_send.at[c, pl.ds(0, OWN * (PEERS - 1))],
-            f_recv.at[:, pl.ds(0, CHUNK * (PEERS - 1)), :],
+            f_recv.at[:, pl.ds(0, PEERS - 1), pl.ds(0, CHUNK), :],
             sends.at[2 + c],
             arrivals.at[2 + c],
             neighbour,
@@ -367,7 +367,7 @@
         f_self.append(
             pltpu.make_async_copy(
                 f_send.at[c, pl.ds(OWN * me, OWN)],
-                f_recv.at[:, pl.ds(pl.multiple_of(me * SENSORS + c * CHUNK, CHUNK), CHUNK), :],
+                f_recv.at[:, me, pl.ds(c * CHUNK, CHUNK), :],
                 self_sems.at[1 + c],
             )
         )
@@ -381,26 +381,44 @@
     for dd in range(OWN):
         gh_ref[dd] = dot(down2[dd], u_recv[dd]).T
 
+    pres = tuple(jnp.zeros((PATCHES, HIDDEN), F32) for _ in range(OWN))
     for c in range(CHUNKS):
         f_self[c].wait()
         f_all[c].wait_recv()
-
+        rows = pl.ds(c * CHUNK, CHUNK)
+        many = 256 // CHUNK
+
+        def mix(b, pres):
+            at = pl.ds(b * many, many)
+            return tuple(
+                pre
+                + dot(
+                    f_recv[dd, at, rows, :].reshape(256, PATCHES),
+                    up2[dd, at, rows, :].reshape(256, HIDDEN),
+                    TN,
+                )
+                for dd, pre in enumerate(pres)
+            )
+
+        pres = lax.fori_loop(0, PEERS // many, mix, pres)
+
+    def project(b, lows):
+        at = pl.ds(pl.multiple_of(b * 256, 256), 256)
+        return tuple(
+            low + dot(df2_ref[:, at], f_recv[dd, pl.ds(b * 4, 4)].reshape(256, PATCHES))
+            for dd, low in enumerate(lows)
+        )
+
+    lows = lax.fori_loop(
+        0,
+        SLOTS // 256,
+        project,
+        tuple(jnp.zeros((8, PATCHES), F32) for _ in range(OWN)),
+        unroll=4,
+    )
     for dd in range(OWN):
-
-        def mix(b, carry):
-            pre, low = carry
-            at = pl.ds(pl.multiple_of(b * 256, 256), 256)
-            f = f_recv[dd, at, :]
-            return pre + dot(f, up2[dd, at, :], TN), low + dot(df2_ref[:, at], f)
-
-        pre, low = lax.fori_loop(
-            0,
-            SLOTS // 256,
-            mix,
-            (jnp.zeros((PATCHES, HIDDEN), F32), jnp.zeros((8, PATCHES), F32)),
-            unroll=2,
-        )
-        low = low.astype(BF16)
+        pre = pres[dd]
+        low = lows[dd].astype(BF16)
         value, slope = gelu_parts(pre + dot(low, uf2_ref[...], TN))
         hid_ref[dd] = value.astype(BF16)
         gp2 = (gh_ref[dd] * slope).astype(BF16)
@@ -475,8 +493,10 @@
         at = pl.ds(pl.multiple_of(chip * 128, 128), 128)
         gd2 = []
         for dd in range(OWN):
-            grad = dot(up2[dd, at, :], gp2_ref[dd], NT) + dot(df2_ref[:, at], back_ref[dd], TN)
-            gd2.append(dot(back_ref[dd], f_recv[dd, at, :], NT))
+            grad = dot(up2[dd, pl.ds(2 * chip, 2)].reshape(128, HIDDEN), gp2_ref[dd], NT) + dot(df2_ref[:, at], back_ref[dd], TN)
+            gd2.append(
+                dot(back_ref[dd], f_recv[dd, pl.ds(2 * chip, 2)].reshape(128, PATCHES), NT)
+            )
             grad = grad.astype(BF16)
             for part_of in range(4):
                 core, half = part_of // 2, part_of % 2
@@ -728,7 +748,7 @@
             pltpu.VMEM((TAPS, SENSORS, CHANNELS), BF16),
             pltpu.VMEM((SENSORS, CHANNELS, HIDDEN), BF16),
             pltpu.VMEM((SENSORS, CHANNELS, HIDDEN), BF16),
-            pltpu.VMEM((OWN, SLOTS, HIDDEN), BF16),
+            pltpu.VMEM((OWN, PEERS, SENSORS, HIDDEN), BF16),
             pltpu.VMEM((OWN, HIDDEN, SLOTS), BF16),
             pltpu.VMEM((SENSORS, CHANNELS, PATCHES), BF16),
             pltpu.VMEM((GROUPS, PADDED * 8, 128), F32),
@@ -741,7 +761,7 @@
             pltpu.VMEM((CHANNELS, SENSORS, PATCHES), BF16),
             pltpu.VMEM((OWN, SLOTS, PATCHES), BF16),
             pltpu.VMEM((CHUNKS, CHANNELS, CHUNK, PATCHES), BF16),
-            pltpu.VMEM((OWN, SLOTS, PATCHES), BF16),
+            pltpu.VMEM((OWN, PEERS, SENSORS, PATCHES), BF16),
             pltpu.VMEM((HALVES, PEERS, OWN, BATCH, PATCHES), BF16),
             pltpu.VMEM((HALVES, CHANNELS, BATCH, PATCHES), BF16),
             pltpu.VMEM((PEERS, OWN, SENSORS, PATCHES), BF16),
@@ -780,7 +800,7 @@
         jnp.transpose(depthwise_weight, (2, 0, 1)),
         channel_up_weight,
         jnp.transpose(channel_down_weight, (0, 2, 1)),
-        sensor_up_weight,
+        sensor_up_weight.reshape(OWN, PEERS, SENSORS, HIDDEN),
         sensor_down_weight,
         upstream[0],
     )

time: 88.6 us -> 87.5 us (0.988)
  Pallas kernels: 87 us -> 85.9 us
    pallas_call x1, Pallas kernels: 83.5 us -> 82.4 us  [body(): pl.pallas_call(kernel, out_shape=(jax.ShapeDtypeStruct((CHANNELS, SENSORS...]
where the time goes in v6:
time: 87.5 us; the launch traced here: 87.3 us
  Pallas kernels  85.9 us (98%)
  between operations  1.45 us (2%)
    pallas_call x1, Pallas kernels, body(): pl.pallas_call(kernel, out_shape=(jax.ShapeDtypeStruct((CHANNELS, SENSORS...  82.4 us
    pallas_call x1, Pallas kernels, body(): pl.pallas_call(finish, out_shape=(jax.ShapeDtypeStruct((SENSORS, CHANNELS...  3.43 us

profile of v6, /device:TPU:1, one launch (start us, length us, event | category | flops | bytes accessed | tf_op | source)
XLA Modules:
  0.0 87.3 jit_solution(11419913875593046084)
XLA Ops:
  1.3 82.4 %shard_map.173 = (bf16[64,64,128]{2,1,0:T(8,128)(2,1)}, f32[21,8,128]{2,1,0:T(8,128)}) custom-call(s32[1]{0:T(128)S(6)} %copy.19.count_ref, f32[1,64]{1,0:T(1,128)} %bitcast.20, f32[1,64]{1,0:T(1,128)} %bitcast.21, bf16[8,64]{1,0:T(8,128)(2,1)} %bitcast.19, bf16[8,256]{1,0:T(8,128)(2,1)} %uf1_ref.1, bf16[8,2048]{1,0:T(8,128)(2,1)} %bitcast.18, ...), custom_call_target="tpu_custom_call" | custom-call | flops 2000000000 | bytes 12000000 | tf_op jit(solution)/shard_map/pallas_call | solution.py:738
  83.7 3.4 %shard_map.174 = (bf16[64,64,128]{2,1,0:T(8,128)(2,1)}, f32[8,64]{1,0:T(8,128)}, f32[8,256]{1,0:T(8,128)}, f32[8,2048]{1,0:T(8,128)}, f32[8,256]{1,0:T(8,128)}) custom-call(s32[1]{0:T(128)S(6)} %copy.19.count_ref, bf16[64,64,128]{2,1,0:T(8,128)(2,1)} %bitcast.13, bf16[64,64,128]{2,1,0:T(8,128)(2,1)} %get-tuple-element.12.received_hbm, ...), custom_call_target="tpu_custom_call" | custom-call | tf_op jit(solution)/shard_map/pallas_call | solution.py:807
